TPU v7x, 1024 devices: a whole 8x8x8 slice. The times are simulated.
1024 devices in a mesh: blk: 64 (over z, y), rep: 16 (over x, core).
Axes of the slice: x: 8, y: 8, z: 8, core: 2. Of those that a mesh axis runs over, the one named last changes fastest.
Arguments:
- features: bfloat16 [32768, 256], P('blk'), may hold values from -6 to 6
- weight: bfloat16 [256, 256], replicated, may hold values from -0.375 to 0.375
- cotangent: bfloat16 [32768, 256], P(('blk', 'rep')), may hold values from -6 to 6
- tile_values: bfloat16 [64, 64, 12, 128, 128], P('blk', 'rep'), may hold values from -0.0546875 to 0.0546875
- tile_rows: int32 [64, 64, 12], P('blk', 'rep'), may hold values from 0 to 3, as said below
- tile_cols: int32 [64, 64, 12], P('blk', 'rep'), may hold values from 0 to 3
- tile_count: int32 [64, 64], P('blk', 'rep'), may hold values from 1 to 12, as said below
Outputs:
- activations: bfloat16 [32768, 256], P(('blk', 'rep'))
- weight_grad: float32 [256, 256], replicated
- feature_grad: bfloat16 [32768, 256], P(('blk', 'rep'))
Inputs may be any that keep to these rules, and one draw needn't show every extreme that they name: Among the live slots of one list the pairs (tile_rows, tile_cols) are distinct. `tile_count`: the list of a block with itself (offset 0) always has 12 live slots.
All inputs are finite; a program needn't handle non-finite values.
Results may differ from a plain program's by a relative error of at most 0.024.
Values may be sent and summed in bfloat16 or wider, within the bound.
No kernel may reach another device: no remote copies, remote signals or barrier semaphores. Data moves between devices by JAX's collectives and lax.ppermute only.
A program may use at most 32 MiB of HBM per device.

v0:
```python
import math

import jax
import jax.numpy as jnp
from jax import lax
from jax.sharding import PartitionSpec as P


def from_behind(shard, axis, by):
    size = lax.axis_size(axis)
    return lax.ppermute(shard, axis, [(i, (i + by) % size) for i in range(size)])


def dense_block(tiles, rows, cols, count, rows_blk):
    row_tiles = rows_blk // 128
    live = jnp.arange(tiles.shape[0], dtype=jnp.int32) < count
    targets = jnp.arange(row_tiles, dtype=jnp.int32)
    col_hot = ((cols[:, None] == targets[None, :]) & live[:, None]).astype(jnp.bfloat16)
    row_hot = (rows[:, None] == targets[None, :]).astype(jnp.bfloat16)
    placed = jnp.einsum("sc,sij->sicj", col_hot, tiles, preferred_element_type=jnp.float32).astype(
        jnp.bfloat16
    )
    placed = placed.reshape(tiles.shape[0], 128, rows_blk)
    whole = jnp.einsum("sr,sik->rik", row_hot, placed, preferred_element_type=jnp.float32).astype(
        jnp.bfloat16
    )
    return whole.reshape(rows_blk, rows_blk)


def forward_padded(tiles, rows, cols, count, block):
    matrix = dense_block(tiles, rows, cols, count, block.shape[0])
    return jnp.dot(matrix, block, preferred_element_type=jnp.float32)


def backward_padded(tiles, rows, cols, count, grads):
    matrix = dense_block(tiles, rows, cols, count, grads.shape[0])
    return lax.dot_general(
        matrix, grads, (((0,), (0,)), ((), ())), preferred_element_type=jnp.float32
    )


def silu_parts(z_value, cot_rows):
    sigma = jax.nn.sigmoid(z_value)
    output = (z_value * sigma).astype(jnp.bfloat16)
    slope = (cot_rows.astype(jnp.float32) * sigma * (1.0 + z_value * (1.0 - sigma))).astype(
        jnp.bfloat16
    )
    return (output, slope)


def per_device(features, weight, cotangent, tile_values, tile_rows, tile_cols, tile_count):
    rows_blk, width = features.shape
    sections = tile_count.shape[1]
    replicas = lax.axis_size("rep")
    rep_index = lax.axis_index("rep")
    bit_count = replicas.bit_length() - 1
    nodes = rows_blk * lax.axis_size("blk")
    block = features
    for bit in range(bit_count):
        moved = from_behind(block, "blk", -(sections << bit))
        block = jnp.where(rep_index >> bit & 1 == 1, moved, block)
    partial_value = jnp.zeros((rows_blk, width), jnp.float32)
    for section in range(sections):
        partial_value = partial_value + forward_padded(
            tile_values[0, section],
            tile_rows[0, section],
            tile_cols[0, section],
            tile_count[0, section],
            block,
        )
        if section + 1 < sections:
            block = from_behind(block, "blk", -1)
    agg = lax.psum_scatter(partial_value, "rep", scatter_dimension=0, tiled=True).astype(
        jnp.bfloat16
    )
    z_value = jnp.dot(agg, weight, preferred_element_type=jnp.float32)
    activations, dz_value = silu_parts(z_value, cotangent)
    weight_term = jnp.dot(agg.T, dz_value, preferred_element_type=jnp.float32)
    dy_rows = jnp.dot(dz_value, weight.T, preferred_element_type=jnp.float32).astype(jnp.bfloat16)
    dy_block = lax.all_gather(dy_rows, "rep", axis=0, tiled=True)
    weight_grad = lax.psum(weight_term, ("blk", "rep")) / math.sqrt(nodes)
    carried = jnp.zeros((rows_blk, width), jnp.float32)
    for section in reversed(range(sections)):
        carried = carried + backward_padded(
            tile_values[0, section],
            tile_rows[0, section],
            tile_cols[0, section],
            tile_count[0, section],
            dy_block,
        )
        if section > 0:
            carried = from_behind(carried, "blk", 1)
    for bit in range(bit_count):
        moved = from_behind(carried.astype(jnp.bfloat16), "blk", sections << bit).astype(
            carried.dtype
        )
        carried = jnp.where(rep_index >> bit & 1 == 1, moved, carried)
    feature_grad = lax.psum_scatter(
        carried.astype(jnp.bfloat16), "rep", scatter_dimension=0, tiled=True
    )
    return (activations, weight_grad, feature_grad)


def solution(mesh):
    return jax.shard_map(
        per_device,
        mesh=mesh,
        in_specs=(
            P("blk", None),
            P(),
            P(("blk", "rep"), None),
            P("blk", "rep", None, None, None),
            P("blk", "rep", None),
            P("blk", "rep", None),
            P("blk", "rep"),
        ),
        out_specs=(P(("blk", "rep"), None), P(), P(("blk", "rep"), None)),
        check_vma=False,
    )
```

profile of v0, /device:TPU:1, one launch (start us, length us, event | category | flops | bytes accessed | tf_op | source)
XLA Modules:
  0.0 668.3 jit_solution(15948597599336071548)
XLA Ops:
  7.2 23.6 %collective-permute-start = (bf16[512,256]{1,0:T(8,128)(2,1)}, bf16[512,256]{1,0:T(8,128)(2,1)S(1)}, u32[]{:S(2)}, u32[]{:S(2)}) collective-permute-start(bf16[512,256]{1,0:T(8,128)(2,1)} %param.7), channel_id=1, source_target_pairs={{0,960},{16,976},{32,992},{48,1008},{64,0},{80,16},{96,32},{112,48... | collective-permute-start | bytes 786440 | tf_op jit(solution)/shard_map/ppermute | solution.py:11
  30.8 1.4 fusion.26
  34.4 2.9 bitcast_convert_fusion
  37.7 1.5 multiply_convert_fusion.2
  39.2 3.5 copy.18
  43.3 1.2 copy.14
  44.4 2.6 multiply_convert_fusion.3
  47.0 4.5 copy.15
  51.5 1.3 iota_compare_fusion.8
  55.8 1.9 collective-permute-start.1
  57.7 1.5 multiply_convert_fusion.1
  59.3 3.5 copy.21
  62.8 1.8 collective-permute-done.1
  64.6 1.9 collective-permute-start.2
  67.1 1.4 copy.23
  68.5 10.6 %collective-permute-done.2 = bf16[512,256]{1,0:T(8,128)(2,1)} collective-permute-done((bf16[512,256]{1,0:T(8,128)(2,1)S(1)}, bf16[512,256]{1,0:T(8,128)(2,1)}, u32[]{:S(2)}, u32[]{:S(2)}) %collective-permute-start.2) | collective-permute-done | bytes 262176 | tf_op jit(solution)/shard_map/ppermute | solution.py:11
  79.9 1.9 collective-permute-start.3
  81.8 1.5 multiply_convert_fusion
  83.3 3.5 copy.24
  86.8 4.3 collective-permute-done.3
  91.2 1.0 broadcast_select_fusion.3
  92.2 12.4 %collective-permute-start.4 = (bf16[512,256]{1,0:T(8,128)(2,1)S(1)}, bf16[512,256]{1,0:T(8,128)(2,1)S(1)}, u32[]{:S(2)}, u32[]{:S(2)}) collective-permute-start(bf16[512,256]{1,0:T(8,128)(2,1)S(1)} %broadcast_select_fusion.3), channel_id=1, source_target_pairs={{0,1008},{16,0},{32,16},{48,32},{64,48},{80,64},{96,80},{112,96},{... | collective-permute-start | bytes 786440 | tf_op jit(solution)/shard_map/ppermute | solution.py:11
  105.2 3.3 collective-permute-done.4
  108.5 7.4 %collective-permute-start.5 = (bf16[512,256]{1,0:T(8,128)(2,1)S(1)}, bf16[512,256]{1,0:T(8,128)(2,1)S(1)}, u32[]{:S(2)}, u32[]{:S(2)}) collective-permute-start(bf16[512,256]{1,0:T(8,128)(2,1)S(1)} %collective-permute-done.4), channel_id=1, source_target_pairs={{0,1008},{16,0},{32,16},{48,32},{64,48},{80,64},{96,80},{112,96},{... | collective-permute-start | bytes 786440 | tf_op jit(solution)/shard_map/ppermute | solution.py:11
  116.5 2.7 collective-permute-done.5
  119.2 7.1 %collective-permute-start.6 = (bf16[512,256]{1,0:T(8,128)(2,1)S(1)}, bf16[512,256]{1,0:T(8,128)(2,1)S(1)}, u32[]{:S(2)}, u32[]{:S(2)}) collective-permute-start(bf16[512,256]{1,0:T(8,128)(2,1)S(1)} %collective-permute-done.5), channel_id=1, source_target_pairs={{0,1008},{16,0},{32,16},{48,32},{64,48},{80,64},{96,80},{112,96},{... | collective-permute-start | bytes 786440 | tf_op jit(solution)/shard_map/ppermute | solution.py:11
  126.6 3.0 collective-permute-done.6
  129.6 1.1 convolution_add_fusion.1
  130.8 69.5 %reduce-scatter.3.cloned.1.call-done = f32[32,256]{1,0:T(8,128)} async-done(((f32[512,256]{1,0:T(8,128)}), f32[32,256]{1,0:T(8,128)}) %reduce-scatter.3.cloned.1.call-update) | async-done | bytes 32784 | tf_op jit(solution)/shard_map/reduce_scatter | solution.py:73
  200.3 1.5 multiply_convert_fusion.5
  202.0 15.5 %all_gather.3 = bf16[512,256]{1,0:T(8,128)(2,1)S(1)} all-gather(bf16[32,256]{1,0:T(8,128)(2,1)S(1)} %convolution_convert_fusion.4), channel_id=1, replica_groups=mesh['blk'=64,'rep'=16] {'rep'}, dimensions={0}, use_global_device_ids=true | all-gather | bytes 278528 | tf_op jit(solution)/shard_map/all_gather | solution.py:80
  217.9 3.1 collective-permute-start.7
  221.0 18.3 %collective-permute-done.7 = f32[512,256]{1,0:T(8,128)S(1)} collective-permute-done((f32[512,256]{1,0:T(8,128)S(1)}, f32[512,256]{1,0:T(8,128)S(1)}, u32[]{:S(2)}, u32[]{:S(2)}) %collective-permute-start.7) | collective-permute-done | bytes 524320 | tf_op jit(solution)/shard_map/ppermute | solution.py:11
  239.6 1.9 collective-permute-start.8
  241.9 15.8 %collective-permute-done.8 = f32[512,256]{1,0:T(8,128)S(1)} collective-permute-done((f32[512,256]{1,0:T(8,128)S(1)}, f32[512,256]{1,0:T(8,128)S(1)}, u32[]{:S(2)}, u32[]{:S(2)}) %collective-permute-start.8) | collective-permute-done | bytes 524320 | tf_op jit(solution)/shard_map/ppermute | solution.py:11
  257.7 1.9 collective-permute-start.9
  260.0 14.8 %collective-permute-done.9 = f32[512,256]{1,0:T(8,128)S(1)} collective-permute-done((f32[512,256]{1,0:T(8,128)S(1)}, f32[512,256]{1,0:T(8,128)S(1)}, u32[]{:S(2)}, u32[]{:S(2)}) %collective-permute-start.9) | collective-permute-done | bytes 524320 | tf_op jit(solution)/shard_map/ppermute | solution.py:11
  274.9 1.9 collective-permute-start.10
  276.9 11.2 %collective-permute-done.10 = bf16[512,256]{1,0:T(8,128)(2,1)S(1)} collective-permute-done((bf16[512,256]{1,0:T(8,128)(2,1)S(1)}, bf16[512,256]{1,0:T(8,128)(2,1)S(1)}, u32[]{:S(2)}, u32[]{:S(2)}) %collective-permute-start.10) | collective-permute-done | bytes 262176 | tf_op jit(solution)/shard_map/ppermute | solution.py:11
  288.1 1.9 collective-permute-start.11
  290.1 6.5 collective-permute-done.11
  296.7 2.0 collective-permute-start.12
  298.7 8.1 %collective-permute-done.12 = bf16[512,256]{1,0:T(8,128)(2,1)S(1)} collective-permute-done((bf16[512,256]{1,0:T(8,128)(2,1)S(1)}, bf16[512,256]{1,0:T(8,128)(2,1)S(1)}, u32[]{:S(2)}, u32[]{:S(2)}) %collective-permute-start.12) | collective-permute-done | bytes 262176 | tf_op jit(solution)/shard_map/ppermute | solution.py:11
  306.9 7.4 %collective-permute-start.13 = (bf16[512,256]{1,0:T(8,128)(2,1)S(1)}, bf16[512,256]{1,0:T(8,128)(2,1)S(1)}, u32[]{:S(2)}, u32[]{:S(2)}) collective-permute-start(bf16[512,256]{1,0:T(8,128)(2,1)S(1)} %fusion.1), channel_id=1, source_target_pairs={{0,512},{16,528},{32,544},{48,560},{64,576},{80,592},{96,608},{112... | collective-permute-start | bytes 786440 | tf_op jit(solution)/shard_map/ppermute | solution.py:11
  315.3 4.2 collective-permute-done.13
  320.3 284.7 %all-reduce.2.cloned.1.call-done = f32[256,256]{1,0:T(8,128)} async-done(((f32[256,256]{1,0:T(8,128)}), f32[256,256]{1,0:T(8,128)}) %all-reduce.2.cloned.1.call-update) | async-done | bytes 262160 | tf_op jit(solution)/shard_map/psum | solution.py:81
  605.0 1.7 broadcast_multiply_fusion
  606.7 55.1 %reduce-scatter.5.cloned.1.call-done = bf16[32,256]{1,0:T(8,128)(2,1)} async-done(((bf16[512,256]{1,0:T(8,128)(2,1)}), bf16[32,256]{1,0:T(8,128)(2,1)}) %reduce-scatter.5.cloned.1.call-update) | async-done | bytes 16400 | tf_op jit(solution)/shard_map/reduce_scatter | solution.py:98
  (66 shorter events, 12.4 us)
Async XLA Ops:
  7.2 193.2 %copy-start = (bf16[256,256]{1,0:T(8,128)(2,1)S(1)}, bf16[256,256]{1,0:T(8,128)(2,1)}, u32[]{:S(2)}) copy-start(bf16[256,256]{1,0:T(8,128)(2,1)} %param.8) | copy-start | bytes 393220
  7.2 193.2 %reduce-scatter.3.cloned.1.call-start = ((), (), s32[]{:S(2)}) async-start(), calls=%async_computation.2 | async-start | bytes 557056 | tf_op jit(solution)/shard_map/reduce_scatter | solution.py:73
  7.2 48.5 %collective-permute-start = (bf16[512,256]{1,0:T(8,128)(2,1)}, bf16[512,256]{1,0:T(8,128)(2,1)S(1)}, u32[]{:S(2)}, u32[]{:S(2)}) collective-permute-start(bf16[512,256]{1,0:T(8,128)(2,1)} %param.7), channel_id=1, source_target_pairs={{0,960},{16,976},{32,992},{48,1008},{64,0},{80,16},{96,32},{112,48... | collective-permute-start | bytes 786440 | tf_op jit(solution)/shard_map/ppermute | solution.py:11
  39.2 3.5 copy-start.8
  51.5 1.7 copy-start.1
  53.3 2.1 copy-start.4
  53.7 2.0 copy-start.11
  53.7 2.0 copy-start.5
  55.8 8.7 %collective-permute-start.1 = (bf16[512,256]{1,0:T(8,128)(2,1)S(1)}, bf16[512,256]{1,0:T(8,128)(2,1)S(1)}, u32[]{:S(2)}, u32[]{:S(2)}) collective-permute-start(bf16[512,256]{1,0:T(8,128)(2,1)S(1)} %broadcast_select_fusion), channel_id=1, source_target_pairs={{0,896},{16,912},{32,928},{48,944},{64,960},{80,976},{96,992},{112... | collective-permute-start | bytes 786440 | tf_op jit(solution)/shard_map/ppermute | solution.py:11
  59.3 7.3 %copy-start.10 = (s32[12]{0:T(128)S(1)}, s32[12]{0:T(128)}, u32[]{:S(2)}) copy-start(s32[12]{0:T(128)} %get-tuple-element.10) | copy-start | bytes 148
  64.6 14.5 %collective-permute-start.2 = (bf16[512,256]{1,0:T(8,128)(2,1)S(1)}, bf16[512,256]{1,0:T(8,128)(2,1)}, u32[]{:S(2)}, u32[]{:S(2)}) collective-permute-start(bf16[512,256]{1,0:T(8,128)(2,1)S(1)} %broadcast_select_fusion.1), channel_id=1, source_target_pairs={{0,768},{16,784},{32,800},{48,816},{64,832},{80,848},{96,864},{112... | collective-permute-start | bytes 786440 | tf_op jit(solution)/shard_map/ppermute | solution.py:11
  79.9 11.3 %collective-permute-start.3 = (bf16[512,256]{1,0:T(8,128)(2,1)}, bf16[512,256]{1,0:T(8,128)(2,1)S(1)}, u32[]{:S(2)}, u32[]{:S(2)}) collective-permute-start(bf16[512,256]{1,0:T(8,128)(2,1)} %broadcast_select_fusion.2), channel_id=1, source_target_pairs={{0,512},{16,528},{32,544},{48,560},{64,576},{80,592},{96,608},{112... | collective-permute-start | bytes 786440 | tf_op jit(solution)/shard_map/ppermute | solution.py:11
  83.3 21.3 %copy-start.9 = (s32[12]{0:T(128)S(1)}, s32[12]{0:T(128)}, u32[]{:S(2)}) copy-start(s32[12]{0:T(128)} %get-tuple-element.7) | copy-start | bytes 148
  86.8 29.1 %copy-start.2 = (bf16[4,128,512]{2,1,0:T(8,128)(2,1)S(1)}, bf16[4,128,512]{2,1,0:T(8,128)(2,1)}, u32[]{:S(2)}) copy-start(bf16[4,128,512]{2,1,0:T(8,128)(2,1)} %copy.19) | copy-start | bytes 1572868
  92.2 16.3 %collective-permute-start.4 = (bf16[512,256]{1,0:T(8,128)(2,1)S(1)}, bf16[512,256]{1,0:T(8,128)(2,1)S(1)}, u32[]{:S(2)}, u32[]{:S(2)}) collective-permute-start(bf16[512,256]{1,0:T(8,128)(2,1)S(1)} %broadcast_select_fusion.3), channel_id=1, source_target_pairs={{0,1008},{16,0},{32,16},{48,32},{64,48},{80,64},{96,80},{112,96},{... | collective-permute-start | bytes 786440 | tf_op jit(solution)/shard_map/ppermute | solution.py:11
  108.5 10.7 %collective-permute-start.5 = (bf16[512,256]{1,0:T(8,128)(2,1)S(1)}, bf16[512,256]{1,0:T(8,128)(2,1)S(1)}, u32[]{:S(2)}, u32[]{:S(2)}) collective-permute-start(bf16[512,256]{1,0:T(8,128)(2,1)S(1)} %collective-permute-done.4), channel_id=1, source_target_pairs={{0,1008},{16,0},{32,16},{48,32},{64,48},{80,64},{96,80},{112,96},{... | collective-permute-start | bytes 786440 | tf_op jit(solution)/shard_map/ppermute | solution.py:11
  119.2 10.4 %collective-permute-start.6 = (bf16[512,256]{1,0:T(8,128)(2,1)S(1)}, bf16[512,256]{1,0:T(8,128)(2,1)S(1)}, u32[]{:S(2)}, u32[]{:S(2)}) collective-permute-start(bf16[512,256]{1,0:T(8,128)(2,1)S(1)} %collective-permute-done.5), channel_id=1, source_target_pairs={{0,1008},{16,0},{32,16},{48,32},{64,48},{80,64},{96,80},{112,96},{... | collective-permute-start | bytes 786440 | tf_op jit(solution)/shard_map/ppermute | solution.py:11
  126.3 75.5 %copy-start.7 = (bf16[32,256]{1,0:T(8,128)(2,1)S(1)}, bf16[32,256]{1,0:T(8,128)(2,1)}, u32[]{:S(2)}) copy-start(bf16[32,256]{1,0:T(8,128)(2,1)} %param.9) | copy-start | bytes 49156
  130.7 110.9 %copy-start.3 = (bf16[4,128,512]{2,1,0:T(8,128)(2,1)S(1)}, bf16[4,128,512]{2,1,0:T(8,128)(2,1)}, u32[]{:S(2)}) copy-start(bf16[4,128,512]{2,1,0:T(8,128)(2,1)} %copy.19) | copy-start | bytes 1572868
  130.7 474.3 %all-reduce.2.cloned.1.call-start = ((), (), s32[]{:S(2)}) async-start(), calls=%async_computation.3 | async-start | bytes 524288 | tf_op jit(solution)/shard_map/psum | solution.py:81
  217.9 21.4 %collective-permute-start.7 = (f32[512,256]{1,0:T(8,128)S(1)}, f32[512,256]{1,0:T(8,128)S(1)}, u32[]{:S(2)}, u32[]{:S(2)}) collective-permute-start(f32[512,256]{1,0:T(8,128)S(1)} %fusion.28), channel_id=1, source_target_pairs={{0,16},{16,32},{32,48},{48,64},{64,80},{80,96},{96,112},{112,128},... | collective-permute-start | bytes 1572872 | tf_op jit(solution)/shard_map/ppermute | solution.py:11
  239.6 18.0 %collective-permute-start.8 = (f32[512,256]{1,0:T(8,128)S(1)}, f32[512,256]{1,0:T(8,128)S(1)}, u32[]{:S(2)}, u32[]{:S(2)}) collective-permute-start(f32[512,256]{1,0:T(8,128)S(1)} %convolution_add_fusion), channel_id=1, source_target_pairs={{0,16},{16,32},{32,48},{48,64},{64,80},{80,96},{96,112},{112,128},... | collective-permute-start | bytes 1572872 | tf_op jit(solution)/shard_map/ppermute | solution.py:11
  257.7 17.1 %collective-permute-start.9 = (f32[512,256]{1,0:T(8,128)S(1)}, f32[512,256]{1,0:T(8,128)S(1)}, u32[]{:S(2)}, u32[]{:S(2)}) collective-permute-start(f32[512,256]{1,0:T(8,128)S(1)} %add.36), channel_id=1, source_target_pairs={{0,16},{16,32},{32,48},{48,64},{64,80},{80,96},{96,112},{112,128},... | collective-permute-start | bytes 1572872 | tf_op jit(solution)/shard_map/ppermute | solution.py:11
  260.0 54.3 %copy-start.6 = (f32[32,256]{1,0:T(8,128)S(1)}, f32[32,256]{1,0:T(8,128)}, u32[]{:S(2)}) copy-start(f32[32,256]{1,0:T(8,128)} %reduce-scatter.3.cloned.1.call-done) | copy-start | bytes 98308
  274.9 13.1 %collective-permute-start.10 = (bf16[512,256]{1,0:T(8,128)(2,1)S(1)}, bf16[512,256]{1,0:T(8,128)(2,1)S(1)}, u32[]{:S(2)}, u32[]{:S(2)}) collective-permute-start(bf16[512,256]{1,0:T(8,128)(2,1)S(1)} %add.37), channel_id=1, source_target_pairs={{0,64},{16,80},{32,96},{48,112},{64,128},{80,144},{96,160},{112,17... | collective-permute-start | bytes 786440 | tf_op jit(solution)/shard_map/ppermute | solution.py:11
  288.1 8.5 %collective-permute-start.11 = (bf16[512,256]{1,0:T(8,128)(2,1)S(1)}, bf16[512,256]{1,0:T(8,128)(2,1)S(1)}, u32[]{:S(2)}, u32[]{:S(2)}) collective-permute-start(bf16[512,256]{1,0:T(8,128)(2,1)S(1)} %fusion), channel_id=1, source_target_pairs={{0,128},{16,144},{32,160},{48,176},{64,192},{80,208},{96,224},{112... | collective-permute-start | bytes 786440 | tf_op jit(solution)/shard_map/ppermute | solution.py:11
  296.7 10.1 %collective-permute-start.12 = (bf16[512,256]{1,0:T(8,128)(2,1)S(1)}, bf16[512,256]{1,0:T(8,128)(2,1)S(1)}, u32[]{:S(2)}, u32[]{:S(2)}) collective-permute-start(bf16[512,256]{1,0:T(8,128)(2,1)S(1)} %convert_select_fusion.1), channel_id=1, source_target_pairs={{0,256},{16,272},{32,288},{48,304},{64,320},{80,336},{96,352},{112... | collective-permute-start | bytes 786440 | tf_op jit(solution)/shard_map/ppermute | solution.py:11
  306.9 12.6 %collective-permute-start.13 = (bf16[512,256]{1,0:T(8,128)(2,1)S(1)}, bf16[512,256]{1,0:T(8,128)(2,1)S(1)}, u32[]{:S(2)}, u32[]{:S(2)}) collective-permute-start(bf16[512,256]{1,0:T(8,128)(2,1)S(1)} %fusion.1), channel_id=1, source_target_pairs={{0,512},{16,528},{32,544},{48,560},{64,576},{80,592},{96,608},{112... | collective-permute-start | bytes 786440 | tf_op jit(solution)/shard_map/ppermute | solution.py:11
  315.3 346.5 %reduce-scatter.5.cloned.1.call-start = ((), (), s32[]{:S(2)}) async-start(), calls=%async_computation.4 | async-start | bytes 278528 | tf_op jit(solution)/shard_map/reduce_scatter | solution.py:98
Sparse Core Ops, SparseCore 0:
  130.9 69.4 reduce-scatter.2
  315.4 289.5 all-reduce.1
  608.9 52.7 reduce-scatter.4
where the time goes:
time: 669 us; the launch traced here: 668 us
  waiting for transfers between devices  514 us (77%)
  starting transfers between devices  76.7 us (11%)
  local copies, waits for them, and re-layouts  22.1 us (3%)
  other arithmetic  18.1 us (3%)
  blocking collectives  15.5 us (2%)
  between operations  14.2 us (2%)
  matrix products  7.64 us (1%)
    psum x1, waiting for transfers between devices, per_device(): weight_grad = lax.psum(weight_term, ('blk', 'rep')) / math.sqrt(nodes)  285 us
    ppermute x14, waiting for transfers between devices, from_behind(): lax.ppermute(shard, axis, [(i, (i + by) % size) for i in range(size)])  105 us
    ppermute x14, starting transfers between devices, from_behind(): lax.ppermute(shard, axis, [(i, (i + by) % size) for i in range(size)])  76.6 us
    reduce_scatter x1, waiting for transfers between devices, per_device(): lax.psum_scatter(partial_value, 'rep', scatter_dimension=0, tiled=True)  69.5 us
    reduce_scatter x1, waiting for transfers between devices, per_device(): lax.psum_scatter(carried.astype(jnp.bfloat16), 'rep', scatter_dimension=0...  55.1 us
    all_gather x1, blocking collectives, per_device(): dy_block = lax.all_gather(dy_rows, 'rep', axis=0, tiled=True)  15.5 us
    reshape x4, local copies, waits for them, and re-layouts, dense_block(): placed = placed.reshape(tiles.shape[0], 128, rows_blk)  15 us
  transfers between devices with their start and end apart: 17, of which 16 were waited for; matrix products, arithmetic and copies ran while one was open for 6% of the time, Pallas kernels for 0%

commit v1 on v0

v1 whole, which is shorter than its diff:
```python
import math

import jax
import jax.numpy as jnp
from jax import lax
from jax.experimental import pallas as pl
from jax.experimental.pallas import tpu as pltpu
from jax.sharding import Mesh
from jax.sharding import PartitionSpec as P

TILE = 128
BF16 = jnp.bfloat16
F32 = jnp.float32
VMEM = pl.BlockSpec(memory_space=pltpu.VMEM)
SMEM = pl.BlockSpec(memory_space=pltpu.SMEM)
ANY = pl.BlockSpec(memory_space=pl.ANY)


def params(mib=40):
    return pltpu.CompilerParams(vmem_limit_bytes=mib << 20)


def shape_of(shape, dtype=BF16):
    return jax.ShapeDtypeStruct(shape, dtype)


def cost(flops, nbytes):
    return pl.CostEstimate(flops=flops, bytes_accessed=nbytes, transcendentals=0)


def dense_kernel(rows, cols, count, tiles, out):
    section = pl.program_id(0)
    out[...] = jnp.zeros_like(out)
    for slot in range(tiles.shape[1]):

        @pl.when(slot < count[section])
        def _():
            row = pl.multiple_of(rows[section, slot] * TILE, TILE)
            col = pl.multiple_of(cols[section, slot] * TILE, TILE)
            out[0, pl.ds(row, TILE), pl.ds(col, TILE)] = tiles[0, slot]


def dense_blocks(tiles, rows, cols, count, rows_blk):
    sections, slots = tiles.shape[:2]
    return pl.pallas_call(
        dense_kernel,
        grid=(sections,),
        out_shape=shape_of((sections, rows_blk, rows_blk)),
        in_specs=[
            SMEM,
            SMEM,
            SMEM,
            pl.BlockSpec((1, slots, TILE, TILE), lambda i: (i, 0, 0, 0)),
        ],
        out_specs=pl.BlockSpec((1, rows_blk, rows_blk), lambda i: (i, 0, 0)),
        compiler_params=params(),
        cost_estimate=cost(0, tiles.size * 2 + sections * rows_blk * rows_blk * 2),
        name="dense_blocks",
    )(rows, cols, count, tiles)


def window_kernel(pos, planes, out, sems):
    depth, sections = planes.shape[0], out.shape[0]
    first = pos[0] + pos[2]
    copies = []
    for target in range(sections):
        plane = lax.rem(first + (target > pos[1]).astype(jnp.int32), depth)
        copies.append(pltpu.make_async_copy(planes.at[plane], out.at[target], sems.at[target]))
    for copy in copies:
        copy.start()
    for copy in copies:
        copy.wait()


def window_pieces(pos, planes, sections):
    shape = (sections,) + planes.shape[1:]
    return pl.pallas_call(
        window_kernel,
        out_shape=shape_of(shape),
        in_specs=[SMEM, ANY],
        out_specs=ANY,
        scratch_shapes=[pltpu.SemaphoreType.DMA((sections,))],
        compiler_params=params(),
        cost_estimate=cost(0, math.prod(shape) * 4),
        name="window_pieces",
    )(pos, planes)


def block_order(pos, sections, own, section):
    core = pos[3] if own else 1 - pos[3]
    return lax.rem(pos[1] + core * (sections // 2) + section, sections)


def forward_kernel(pos, mine, other, mine_block, other_block, cot, out, total):
    section = pl.program_id(0)
    rows = total.shape[0]
    here = jnp.dot(mine[0], mine_block[0], preferred_element_type=F32) + jnp.dot(
        other[0], other_block[0], preferred_element_type=F32
    )

    @pl.when(section == 0)
    def _():
        total[...] = here

    @pl.when(section > 0)
    def _():
        total[...] += here

    @pl.when(section == pl.num_programs(0) - 1)
    def _():
        half, width = cot.shape[0], out.shape[1]
        out[:rows, :] = total[...].astype(BF16)
        out[rows : rows + half, :] = cot[:, :width]
        out[rows + half :, :] = cot[:, width:]


def forward_part(pos, mine, other, blocks, cot):
    half, rows = mine.shape[:2]
    sections, _, width = blocks.shape
    extra = 2 * cot.shape[0]

    def block_spec(own):
        return pl.BlockSpec(
            (1, rows, width), lambda i, pos: (block_order(pos, sections, own, i), 0, 0)
        )

    matrix = pl.BlockSpec((1, rows, rows), lambda i, pos: (i, 0, 0))
    return pl.pallas_call(
        forward_kernel,
        out_shape=shape_of((rows + extra, width)),
        grid_spec=pltpu.PrefetchScalarGridSpec(
            num_scalar_prefetch=1,
            grid=(half,),
            in_specs=[
                matrix,
                matrix,
                block_spec(True),
                block_spec(False),
                pl.BlockSpec(cot.shape, lambda i, pos: (0, 0)),
            ],
            out_specs=pl.BlockSpec((rows + extra, width), lambda i, pos: (0, 0)),
            scratch_shapes=[pltpu.VMEM((rows, width), F32)],
        ),
        compiler_params=params(),
        cost_estimate=cost(
            2 * sections * rows * rows * width, sections * rows * (rows + width) * 2
        ),
        name="forward_part",
    )(pos, mine, other, blocks, blocks, cot)


def aggregate_kernel(parts, out):
    rows = out.shape[0] // 2
    ranks = parts.shape[0]
    extra = rows // ranks
    total = parts[0, :rows, :].astype(F32)
    for rank in range(1, ranks):
        total += parts[rank, :rows, :].astype(F32)
    out[:rows, :] = total.astype(BF16)
    for rank in range(ranks):
        out[rows + rank * extra : rows + (rank + 1) * extra, :] = parts[rank, rows:, :]


def aggregate_part(parts, rows):
    shape = (2 * rows, parts.shape[2])
    return pl.pallas_call(
        aggregate_kernel,
        out_shape=shape_of(shape),
        in_specs=[VMEM],
        out_specs=VMEM,
        compiler_params=params(),
        cost_estimate=cost(parts.size, parts.size * 2 + math.prod(shape) * 2),
        name="aggregate_part",
    )(parts)


def layer_kernel(ranks, pos, pair, weight, mine, other, act, out, act_all, dz_all, term):
    rows = pair.shape[1] // 2
    width = pair.shape[2]
    own = act.shape[0]
    both = 2 * own
    for rank in range(ranks):
        span = slice(rank * both, (rank + 1) * both)
        z_value = jnp.dot(pair[0, span, :], weight[:width, :], preferred_element_type=F32)
        z_value += jnp.dot(pair[1, span, :], weight[width:, :], preferred_element_type=F32)
        start = rows + rank * both
        cot = jnp.concatenate(
            [
                jnp.concatenate(
                    [pair[core, start + side * own : start + (side + 1) * own, :] for side in (0, 1)],
                    axis=1,
                )
                for core in (0, 1)
            ],
            axis=0,
        ).astype(F32)
        sigma = jax.nn.sigmoid(z_value)
        act_all[span, :] = (z_value * sigma).astype(BF16)
        dz_all[span, :] = (cot * sigma * (1.0 + z_value * (1.0 - sigma))).astype(BF16)
    x_index, core = pos[2], pos[3]
    act[...] = act_all[pl.ds(pl.multiple_of((2 * x_index + core) * own, own), own), :]
    dz_value = dz_all[...]
    contract_rows = (((0,), (0,)), ((), ()))
    contract_cols = (((1,), (1,)), ((), ()))
    term[...] = lax.dot_general(
        pair[core, :rows, :], dz_value, contract_rows, preferred_element_type=F32
    )
    weight_rows = weight[pl.ds(pl.multiple_of(core * width, width), width), :]
    dy_turned = lax.dot_general(
        weight_rows, dz_value, contract_cols, preferred_element_type=F32
    ).astype(BF16)
    chunk = width // ranks
    piece = term[pl.ds(pl.multiple_of(x_index * chunk, chunk), chunk), :].astype(BF16)
    piece = jnp.concatenate([piece[:, :width], piece[:, width:]], axis=0)
    sections = out.shape[0]
    for is_own, matrices in ((True, mine), (False, other)):
        for section in range(sections // 2):
            grads = jnp.dot(dy_turned, matrices[section], preferred_element_type=F32)
            target = block_order(pos, sections, is_own, section)
            out[target, :rows, :] = grads.astype(BF16).T
    for target in range(sections):
        out[target, rows:, :] = piece


def layer_part(pos, pair, weight, mine, other, ranks):
    rows, width = pair.shape[1] // 2, pair.shape[2]
    sections = 2 * mine.shape[0]
    own = rows // (2 * ranks)
    out = (sections, rows + 2 * width // ranks, width)

    def kernel(*refs):
        layer_kernel(ranks, *refs)

    return pl.pallas_call(
        kernel,
        out_shape=(shape_of((own, 2 * width)), shape_of(out)),
        in_specs=[SMEM] + [VMEM] * 4,
        out_specs=(VMEM, VMEM),
        scratch_shapes=[
            pltpu.VMEM((rows, 2 * width), BF16),
            pltpu.VMEM((rows, 2 * width), BF16),
            pltpu.VMEM((width, 2 * width), F32),
        ],
        compiler_params=params(),
        cost_estimate=cost(
            2 * sections * rows * rows * width, mine.size * 4 + math.prod(out) * 2
        ),
        name="layer_part",
    )(pos, pair, weight, mine, other)


def planes_kernel(rows, pos, parts, out):
    sections = parts.shape[0]
    ranks = out.shape[0]
    share = rows // ranks
    for rank in range(ranks):
        span = slice(rank * share, (rank + 1) * share)
        near = jnp.zeros((share, parts.shape[2]), F32)
        far = near
        for source in range(sections):
            value = parts[source, span, :].astype(F32)
            same = source <= pos[1]
            near += jnp.where(same, value, 0.0)
            far += jnp.where(same, 0.0, value)
        out[rank, :share, :] = near.astype(BF16)
        out[rank, share : 2 * share, :] = far.astype(BF16)
    term = parts[0, rows:, :].astype(F32)
    for source in range(1, sections):
        term += parts[source, rows:, :].astype(F32)
    for rank in range(ranks):
        out[rank, 2 * share :, :] = term.astype(BF16)


def planes_part(pos, parts, rows, ranks):
    extra = parts.shape[1] - rows
    shape = (ranks, 2 * rows // ranks + extra, parts.shape[2])

    def kernel(*refs):
        planes_kernel(rows, *refs)

    return pl.pallas_call(
        kernel,
        out_shape=shape_of(shape),
        in_specs=[SMEM, VMEM],
        out_specs=VMEM,
        compiler_params=params(),
        cost_estimate=cost(parts.size * 2, parts.size * 2 + math.prod(shape) * 2),
        name="planes_part",
    )(pos, parts)


def depth_kernel(share, pos, parts, out):
    ranks = parts.shape[0]
    depth = out.shape[0]
    extra = parts.shape[1] - 2 * share
    for target in range(depth):
        near = lax.rem(target - pos[0] + depth, depth)
        far = lax.rem(target - pos[0] + 2 * depth - 1, depth)
        value = parts[near, :share, :].astype(F32) + parts[far, share : 2 * share, :].astype(F32)
        out[target, :share, :] = value.astype(BF16)
        for rank in range(ranks):
            out[target, share + rank * extra : share + (rank + 1) * extra, :] = parts[
                rank, 2 * share :, :
            ]


def depth_part(pos, parts, share, depth):
    ranks, height, width = parts.shape
    shape = (depth, share + ranks * (height - 2 * share), width)

    def kernel(*refs):
        depth_kernel(share, *refs)

    return pl.pallas_call(
        kernel,
        out_shape=shape_of(shape),
        in_specs=[SMEM, VMEM],
        out_specs=VMEM,
        compiler_params=params(),
        cost_estimate=cost(parts.size, parts.size * 2 + math.prod(shape) * 2),
        name="depth_part",
    )(pos, parts)


def total_kernel(parts, out):
    total = parts[0].astype(F32)
    for source in range(1, parts.shape[0]):
        total += parts[source].astype(F32)
    out[...] = total.astype(BF16)


def total_part(parts):
    return pl.pallas_call(
        total_kernel,
        out_shape=shape_of(parts.shape[1:]),
        in_specs=[VMEM],
        out_specs=VMEM,
        compiler_params=params(),
        cost_estimate=cost(parts.size, parts.size * 2),
        name="total_part",
    )(parts)


def finish_kernel(ranks, scale, pos, pair, term, grads):
    width = pair.shape[2]
    own = grads.shape[0]
    start = pl.multiple_of(pos[3] * own, own)
    for core in (0, 1):
        side = slice(core * width, (core + 1) * width)
        grads[:, side] = pair[core, pl.ds(start, own), :]
    chunk = width // ranks
    for core in (0, 1):
        for rank in range(ranks):
            row = core * width + rank * chunk
            for side in (0, 1):
                first = 2 * own + (2 * rank + side) * chunk
                value = pair[core, first : first + chunk, :].astype(F32) / scale
                term[row : row + chunk, side * width : (side + 1) * width] = value


def finish_part(pos, pair, ranks, own, nodes):
    width = pair.shape[2]

    def kernel(*refs):
        finish_kernel(ranks, math.sqrt(nodes), *refs)

    return pl.pallas_call(
        kernel,
        out_shape=(shape_of((2 * width, 2 * width), F32), shape_of((own, 2 * width))),
        in_specs=[SMEM, VMEM],
        out_specs=(VMEM, VMEM),
        compiler_params=params(),
        cost_estimate=cost(0, pair.size * 2),
        name="finish_part",
    )(pos, pair)


def exchange(pieces, axis):
    return lax.all_to_all(pieces, axis, split_axis=0, concat_axis=0, tiled=True)


def per_device(features, weight, cotangent, tile_values, tile_rows, tile_cols, tile_count):
    rows, columns = features.shape
    width = columns // 2
    depth, sections, ranks = lax.axis_size("z"), lax.axis_size("y"), lax.axis_size("x")
    nodes = rows * depth * sections
    own = rows // (2 * ranks)
    core = lax.axis_index("core")
    pos = jnp.stack(
        [lax.axis_index("z"), lax.axis_index("y"), lax.axis_index("x"), core]
    ).astype(jnp.int32)

    mine = dense_blocks(tile_values[0], tile_rows[0], tile_cols[0], tile_count[0], rows)
    other = lax.ppermute(mine, "core", [(0, 1), (1, 0)])

    half = lax.dynamic_slice_in_dim(features, core * width, width, axis=1)
    planes = lax.all_gather(half, "z", axis=0, tiled=False)
    blocks = exchange(window_pieces(pos, planes, sections), "y")
    part = forward_part(pos, mine, other, blocks, cotangent)
    parts = lax.all_gather(part, "x", axis=0, tiled=False)
    pair = lax.all_gather(aggregate_part(parts, rows), "core", axis=0, tiled=False)
    activations, pieces = layer_part(pos, pair, weight, mine, other, ranks)
    pieces = exchange(pieces, "y")
    pieces = exchange(planes_part(pos, pieces, rows, ranks), "x")
    pieces = exchange(depth_part(pos, pieces, rows // ranks, depth), "z")
    pair = lax.all_gather(total_part(pieces), "core", axis=0, tiled=False)
    weight_grad, feature_grad = finish_part(pos, pair, ranks, own, nodes)
    return (activations, weight_grad, feature_grad)


def solution(mesh):
    blk, rep = mesh.devices.shape
    ranks = rep // 2
    devices = mesh.devices.reshape(ranks, blk // ranks, ranks, 2)
    grid = Mesh(devices, ("z", "y", "x", "core"))
    blk_axes, rep_axes = ("z", "y"), ("x", "core")
    return jax.shard_map(
        per_device,
        mesh=grid,
        in_specs=(
            P(blk_axes, None),
            P(),
            P(blk_axes + rep_axes, None),
            P(blk_axes, rep_axes, None, None, None),
            P(blk_axes, rep_axes, None),
            P(blk_axes, rep_axes, None),
            P(blk_axes, rep_axes),
        ),
        out_specs=(P(blk_axes + rep_axes, None), P(), P(blk_axes + rep_axes, None)),
        check_vma=False,
    )
```

time: 669 us -> 244 us (0.36)
  waiting for transfers between devices: 514 us -> 96.3 us
  blocking collectives: 15.5 us -> 87.7 us
  starting transfers between devices: 76.7 us -> 22.8 us
  other arithmetic: 18.1 us -> 0.08 us
  Pallas kernels: 0 us -> 14.3 us
  local copies, waits for them, and re-layouts: 22.1 us -> 8.46 us
  matrix products: 7.64 us -> 0 us
    psum x1 -> x0, waiting for transfers between devices: 285 us -> none  [per_device(): weight_grad = lax.psum(weight_term, ('blk', 'rep')) / math.sqrt(nodes)]
    reduce_scatter x2 -> x0, waiting for transfers between devices: 125 us -> none  [the longest x1 69.5 us: per_device(): lax.psum_scatter(partial_value, 'rep', scatter_dimension=0, tiled=True)]
    ppermute x14 -> x1, waiting for transfers between devices: 105 us -> 0.01 us  [per_device(): other = lax.ppermute(mine, 'core', [(0, 1), (1, 0)])]
    all_to_all x0 -> x3, blocking collectives: none -> 74.4 us  [exchange(): return lax.all_to_all(pieces, axis, split_axis=0, concat_axis=0, tiled=True)]
    all_gather x0 -> x2, waiting for transfers between devices: none -> 71.2 us  [the longest x1 36.6 us: per_device(): parts = lax.all_gather(part, 'x', axis=0, tiled=False)]
    ppermute x14 -> x1, starting transfers between devices: 76.6 us -> 16.1 us  [per_device(): other = lax.ppermute(mine, 'core', [(0, 1), (1, 0)])]
    all_to_all x0 -> x1, waiting for transfers between devices: none -> 25.1 us  [exchange(): return lax.all_to_all(pieces, axis, split_axis=0, concat_axis=0, tiled=True)]
    reshape x4 -> x0, local copies, waits for them, and re-layouts: 15 us -> none  [dense_block(): placed = placed.reshape(tiles.shape[0], 128, rows_blk)]
  transfers between devices with their start and end apart: 17 -> 4, of which waited for: 16 -> 3; matrix products, arithmetic and copies ran while one was open for 6% -> 0% of each run, Pallas kernels for 0% -> 1%
where the time goes in v1:
time: 244 us
  waiting for transfers between devices  96.3 us (39%)
  blocking collectives  87.7 us (36%)
  starting transfers between devices  22.8 us (9%)
  Pallas kernels  14.3 us (6%)
  between operations  14.1 us (6%)
  local copies, waits for them, and re-layouts  8.46 us (3%)
    all_to_all x3, blocking collectives, exchange(): return lax.all_to_all(pieces, axis, split_axis=0, concat_axis=0, tiled=True)  74.4 us
    all_gather x1, waiting for transfers between devices, per_device(): parts = lax.all_gather(part, 'x', axis=0, tiled=False)  36.6 us
    all_gather x1, waiting for transfers between devices, per_device(): planes = lax.all_gather(half, 'z', axis=0, tiled=False)  34.6 us
    all_to_all x1, waiting for transfers between devices, exchange(): return lax.all_to_all(pieces, axis, split_axis=0, concat_axis=0, tiled=True)  25.1 us
    ppermute x1, starting transfers between devices, per_device(): other = lax.ppermute(mine, 'core', [(0, 1), (1, 0)])  16.1 us
    unnamed x20, local copies, waits for them, and re-layouts  7.79 us
    all_to_all x1, starting transfers between devices, exchange(): return lax.all_to_all(pieces, axis, split_axis=0, concat_axis=0, tiled=True)  6.68 us
    all_gather x1, blocking collectives, per_device(): lax.all_gather(aggregate_part(parts, rows), 'core', axis=0, tiled=False)  6.66 us
  transfers between devices with their start and end apart: 4, of which 3 were waited for; matrix products, arithmetic and copies ran while one was open for 0% of the time, Pallas kernels for 1%

profile of v1, /device:TPU:1, one launch (start us, length us, event | category | flops | bytes accessed | tf_op | source)
XLA Modules:
  0.0 243.8 jit_solution(13001452565865648006)
XLA Ops:
  7.2 0.0 copy-start
  7.2 0.0 all-gather.7.cloned.1.call-start
  7.2 0.9 copy-done
  8.1 0.7 constant_dynamic-slice_fusion
  8.8 0.0 all-gather.7.cloned.1.call-update
  8.8 0.0 copy-start.2
  8.8 1.4 copy-done.2
  10.2 0.0 copy-start.7
  10.2 0.7 copy-done.7
  10.9 0.0 copy-start.8
  10.9 0.7 copy-done.8
  11.6 0.0 copy-start.9
  11.6 0.7 copy-done.9
  12.2 1.4 dense_blocks.1.mine.refs_3_
  13.7 16.1 %collective-permute-start = (bf16[4,512,512]{2,1,0:T(8,128)(2,1)S(1)}, bf16[4,512,512]{2,1,0:T(8,128)(2,1)}, u32[]{:S(2)}, u32[]{:S(2)}) collective-permute-start(bf16[4,512,512]{2,1,0:T(8,128)(2,1)S(1)} %dense_blocks.1.mine.refs_3_), channel_id=1, source_target_pairs={{0,1},{1,0},{2,3},{3,2},{4,5},{5,4},{6,7},{7,6},{8,9},{9,8},{10,11... | collective-permute-start | bytes 6291464 | tf_op jit(solution)/shard_map/ppermute | solution.py:394
  29.8 0.1 pad_add_fusion.pos.refs_0_
  29.9 34.6 %all-gather.7.cloned.1.call-done = bf16[4096,128]{1,0:T(8,128)(2,1)} async-done(((bf16[512,128]{1,0:T(8,128)(2,1)}), bf16[4096,128]{1,0:T(8,128)(2,1)}) %all-gather.7.cloned.1.call-update) | async-done | bytes 1048592 | tf_op jit(solution)/shard_map/all_gather | solution.py:397
  64.5 0.0 copy-start.4
  64.5 1.2 copy-done.4
  65.7 2.0 window_pieces.1
  67.7 0.0 copy-start.1
  67.7 1.0 copy-done.1
  68.7 0.0 copy-start.6
  68.7 6.7 %all-to-all-start = ((bf16[8,512,128]{2,1,0:T(8,128)(2,1)}), bf16[8,512,128]{2,1,0:T(8,128)(2,1)S(1)}, u32[]{:S(2)}, u32[]{:S(2)}) async-start(bf16[8,512,128]{2,1,0:T(8,128)(2,1)} %copy-done.1), calls=%async_computation | async-start | bytes 2097152 | tf_op jit(solution)/shard_map/all_to_all | solution.py:379
  75.4 0.0 all-gather.9.cloned.1.call-start
  75.4 0.0 collective-permute-done.other.refs_4_
  75.4 25.1 %all-to-all-done.mine_block.other_block = bf16[8,512,128]{2,1,0:T(8,128)(2,1)S(1)} async-done(((bf16[8,512,128]{2,1,0:T(8,128)(2,1)}), bf16[8,512,128]{2,1,0:T(8,128)(2,1)S(1)}, u32[]{:S(2)}, u32[]{:S(2)}) %all-to-all-start) | async-done | bytes 1048608 | tf_op jit(solution)/shard_map/all_to_all | solution.py:379
  100.5 0.0 copy-done.6
  100.5 4.8 %forward_part.1 = bf16[576,128]{1,0:T(8,128)(2,1)} custom-call(s32[4]{0:T(128)S(1)} %pad_add_fusion.pos.refs_0_, bf16[4,512,512]{2,1,0:T(8,128)(2,1)S(1)} %dense_blocks.1.mine.refs_3_, bf16[4,512,512]{2,1,0:T(8,128)(2,1)} %collective-permute-done.other.refs_4_, bf16[8,512,128]{2,1,0:T(8,128)(2,1)S(1)} %all-to-all-done.mine_block.other_block, ...), custom_call_target="tpu_custom_call" | custom-call | flops 536870912 | bytes 5242880 | tf_op jit(solution)/shard_map/forward_part/pallas_call | solution.py:128
  105.2 0.0 copy-start.5
  105.3 0.0 all-gather.9.cloned.1.call-update
  105.3 36.6 %all-gather.9.cloned.1.call-done = bf16[4608,128]{1,0:T(8,128)(2,1)} async-done(((bf16[576,128]{1,0:T(8,128)(2,1)}), bf16[4608,128]{1,0:T(8,128)(2,1)}) %all-gather.9.cloned.1.call-update) | async-done | bytes 1179664 | tf_op jit(solution)/shard_map/all_gather | solution.py:400
  141.9 0.0 copy-start.3
  141.9 1.3 copy-done.3
  143.2 0.1 aggregate_part.1
  143.3 6.7 %all-gather.2 = bf16[2048,128]{1,0:T(8,128)(2,1)S(1)} all-gather(bf16[1024,128]{1,0:T(8,128)(2,1)S(1)} %aggregate_part.1), channel_id=4, replica_groups=mesh['z'=8,'y'=8,'x'=8,'core'=2] {'core'}, dimensions={0}, use_global_device_ids=true | all-gather | bytes 786432 | tf_op jit(solution)/shard_map/all_gather | solution.py:401
  150.0 0.0 copy-done.5
  150.0 3.0 %layer_part.1 = (bf16[32,256]{1,0:T(8,128)(2,1)}, bf16[8,544,128]{2,1,0:T(8,128)(2,1)S(1)}) custom-call(s32[4]{0:T(128)S(1)} %pad_add_fusion.pos.refs_0_, bf16[2,1024,128]{2,1,0:T(8,128)(2,1)S(1)} %bitcast.12, bf16[256,256]{1,0:T(8,128)(2,1)S(1)} %copy-done.5, bf16[4,512,512]{2,1,0:T(8,128)(2,1)S(1)} %dense_blocks.1.mine.refs_3_, ...), custom_call_target="tpu_custom_call" | custom-call | flops 536870912 | bytes 5308416 | tf_op jit(solution)/shard_map/layer_part/pallas_call | solution.py:234
  153.0 36.0 %all_to_all.20.refs_1_ = bf16[8,544,128]{2,1,0:T(8,128)(2,1)S(1)} all-to-all(bf16[8,544,128]{2,1,0:T(8,128)(2,1)S(1)} %get-tuple-element.8), channel_id=1, replica_groups=mesh['z'=8,'y'=8,'x'=8,'core'=2] {'y'}, dimensions={0} | all-to-all | bytes 2228224 | tf_op jit(solution)/shard_map/all_to_all | solution.py:379
  188.9 0.9 planes_part.1
  189.9 14.6 %all_to_all.21.refs_1_ = bf16[8,160,128]{2,1,0:T(8,128)(2,1)S(1)} all-to-all(bf16[8,160,128]{2,1,0:T(8,128)(2,1)S(1)} %planes_part.1), channel_id=1, replica_groups=mesh['z'=8,'y'=8,'x'=8,'core'=2] {'x'}, dimensions={0} | all-to-all | bytes 655360 | tf_op jit(solution)/shard_map/all_to_all | solution.py:379
  204.5 0.6 depth_part.1
  205.1 23.9 %all_to_all.22.parts = bf16[8,320,128]{2,1,0:T(8,128)(2,1)S(1)} all-to-all(bf16[8,320,128]{2,1,0:T(8,128)(2,1)S(1)} %depth_part.1), channel_id=1, replica_groups=mesh['z'=8,'y'=8,'x'=8,'core'=2] {'z'}, dimensions={0} | all-to-all | bytes 1310720 | tf_op jit(solution)/shard_map/all_to_all | solution.py:379
  229.0 0.1 total_part.1
  229.1 6.6 %all-gather.3 = bf16[640,128]{1,0:T(8,128)(2,1)S(1)} all-gather(bf16[320,128]{1,0:T(8,128)(2,1)S(1)} %total_part.1), channel_id=5, replica_groups=mesh['z'=8,'y'=8,'x'=8,'core'=2] {'core'}, dimensions={0}, use_global_device_ids=true | all-gather | bytes 245760 | tf_op jit(solution)/shard_map/all_gather | solution.py:406
  235.7 1.3 finish_part.1
Async XLA Ops:
  7.2 1.0 copy-start
  7.2 57.3 %all-gather.7.cloned.1.call-start = ((), (), s32[]{:S(2)}) async-start(), calls=%async_computation.4 | async-start | bytes 1179648 | tf_op jit(solution)/shard_map/all_gather | solution.py:397
  8.8 1.4 copy-start.2
  10.2 0.7 copy-start.7
  10.9 0.7 copy-start.8
  11.6 0.7 copy-start.9
  13.7 61.8 %collective-permute-start = (bf16[4,512,512]{2,1,0:T(8,128)(2,1)S(1)}, bf16[4,512,512]{2,1,0:T(8,128)(2,1)}, u32[]{:S(2)}, u32[]{:S(2)}) collective-permute-start(bf16[4,512,512]{2,1,0:T(8,128)(2,1)S(1)} %dense_blocks.1.mine.refs_3_), channel_id=1, source_target_pairs={{0,1},{1,0},{2,3},{3,2},{4,5},{5,4},{6,7},{7,6},{8,9},{9,8},{10,11... | collective-permute-start | bytes 6291464 | tf_op jit(solution)/shard_map/ppermute | solution.py:394
  64.5 1.2 copy-start.4
  67.7 1.0 copy-start.1
  68.7 31.8 %copy-start.6 = (bf16[32,256]{1,0:T(8,128)(2,1)S(1)}, bf16[32,256]{1,0:T(8,128)(2,1)}, u32[]{:S(2)}) copy-start(bf16[32,256]{1,0:T(8,128)(2,1)} %cot.1) | copy-start | bytes 49156
  68.7 31.8 %all-to-all-start = ((bf16[8,512,128]{2,1,0:T(8,128)(2,1)}), bf16[8,512,128]{2,1,0:T(8,128)(2,1)S(1)}, u32[]{:S(2)}, u32[]{:S(2)}) async-start(bf16[8,512,128]{2,1,0:T(8,128)(2,1)} %copy-done.1), calls=%async_computation | async-start | bytes 2097152 | tf_op jit(solution)/shard_map/all_to_all | solution.py:379
  75.4 66.5 %all-gather.9.cloned.1.call-start = ((), (), s32[]{:S(2)}) async-start(), calls=%async_computation.5 | async-start | bytes 1327104 | tf_op jit(solution)/shard_map/all_gather | solution.py:400
  105.2 44.7 %copy-start.5 = (bf16[256,256]{1,0:T(8,128)(2,1)S(1)}, bf16[256,256]{1,0:T(8,128)(2,1)}, u32[]{:S(2)}) copy-start(bf16[256,256]{1,0:T(8,128)(2,1)} %refs_2_.1) | copy-start | bytes 393220
  141.9 1.3 copy-start.3
Sparse Core Ops, SparseCore 0:
  11.2 53.1 all-gather.6
  105.4 36.4 all-gather.8

commit v2 on v1

--- a/solution.py
+++ b/solution.py
@@ -59,29 +59,24 @@
     )(rows, cols, count, tiles)
 
 
-def window_kernel(pos, planes, out, sems):
-    depth, sections = planes.shape[0], out.shape[0]
-    first = pos[0] + pos[2]
-    copies = []
-    for target in range(sections):
-        plane = lax.rem(first + (target > pos[1]).astype(jnp.int32), depth)
-        copies.append(pltpu.make_async_copy(planes.at[plane], out.at[target], sems.at[target]))
-    for copy in copies:
-        copy.start()
-    for copy in copies:
-        copy.wait()
-
-
-def window_pieces(pos, planes, sections):
-    shape = (sections,) + planes.shape[1:]
+def window_kernel(pos, planes, out):
+    depth = planes.shape[0]
+    ranks = depth
+    for target in range(out.shape[0]):
+        ahead = (target // ranks > pos[1]).astype(jnp.int32)
+        plane = lax.rem(pos[0] + target % ranks + ahead, depth)
+        out[target] = planes[plane]
+
+
+def window_pieces(pos, planes, sections, ranks):
+    shape = (sections * ranks,) + planes.shape[1:]
     return pl.pallas_call(
         window_kernel,
         out_shape=shape_of(shape),
-        in_specs=[SMEM, ANY],
-        out_specs=ANY,
-        scratch_shapes=[pltpu.SemaphoreType.DMA((sections,))],
-        compiler_params=params(),
-        cost_estimate=cost(0, math.prod(shape) * 4),
+        in_specs=[SMEM, VMEM],
+        out_specs=VMEM,
+        compiler_params=params(),
+        cost_estimate=cost(0, math.prod(shape) * 2),
         name="window_pieces",
     )(pos, planes)
 
@@ -91,162 +86,130 @@
     return lax.rem(pos[1] + core * (sections // 2) + section, sections)
 
 
-def forward_kernel(pos, mine, other, mine_block, other_block, cot, out, total):
-    section = pl.program_id(0)
-    rows = total.shape[0]
-    here = jnp.dot(mine[0], mine_block[0], preferred_element_type=F32) + jnp.dot(
-        other[0], other_block[0], preferred_element_type=F32
-    )
-
-    @pl.when(section == 0)
-    def _():
-        total[...] = here
-
-    @pl.when(section > 0)
-    def _():
-        total[...] += here
-
-    @pl.when(section == pl.num_programs(0) - 1)
-    def _():
-        half, width = cot.shape[0], out.shape[1]
-        out[:rows, :] = total[...].astype(BF16)
-        out[rows : rows + half, :] = cot[:, :width]
-        out[rows + half :, :] = cot[:, width:]
-
-
-def forward_part(pos, mine, other, blocks, cot):
-    half, rows = mine.shape[:2]
+def fetch(other, held, sem):
+    return pltpu.make_async_copy(other, held, sem)
+
+
+def forward_kernel(pos, mine, other, blocks, out, held, sem):
+    copy = fetch(other, held, sem)
+    copy.start()
+    half = mine.shape[0]
+    sections = blocks.shape[0]
+    total = jnp.zeros(out.shape, F32)
+    for is_own, matrices in ((True, mine), (False, held)):
+        if not is_own:
+            copy.wait()
+        for section in range(half):
+            block = blocks[block_order(pos, sections, is_own, section)]
+            total += jnp.dot(matrices[section], block, preferred_element_type=F32)
+    out[...] = total.astype(BF16)
+
+
+def forward_part(pos, mine, other, blocks):
+    rows = mine.shape[1]
     sections, _, width = blocks.shape
-    extra = 2 * cot.shape[0]
-
-    def block_spec(own):
-        return pl.BlockSpec(
-            (1, rows, width), lambda i, pos: (block_order(pos, sections, own, i), 0, 0)
-        )
-
-    matrix = pl.BlockSpec((1, rows, rows), lambda i, pos: (i, 0, 0))
     return pl.pallas_call(
         forward_kernel,
-        out_shape=shape_of((rows + extra, width)),
-        grid_spec=pltpu.PrefetchScalarGridSpec(
-            num_scalar_prefetch=1,
-            grid=(half,),
-            in_specs=[
-                matrix,
-                matrix,
-                block_spec(True),
-                block_spec(False),
-                pl.BlockSpec(cot.shape, lambda i, pos: (0, 0)),
-            ],
-            out_specs=pl.BlockSpec((rows + extra, width), lambda i, pos: (0, 0)),
-            scratch_shapes=[pltpu.VMEM((rows, width), F32)],
-        ),
+        out_shape=shape_of((rows, width)),
+        in_specs=[SMEM, VMEM, ANY, VMEM],
+        out_specs=VMEM,
+        scratch_shapes=[pltpu.VMEM(other.shape, BF16), pltpu.SemaphoreType.DMA],
         compiler_params=params(),
         cost_estimate=cost(
             2 * sections * rows * rows * width, sections * rows * (rows + width) * 2
         ),
         name="forward_part",
-    )(pos, mine, other, blocks, blocks, cot)
-
-
-def aggregate_kernel(parts, out):
-    rows = out.shape[0] // 2
-    ranks = parts.shape[0]
-    extra = rows // ranks
-    total = parts[0, :rows, :].astype(F32)
-    for rank in range(1, ranks):
-        total += parts[rank, :rows, :].astype(F32)
-    out[:rows, :] = total.astype(BF16)
-    for rank in range(ranks):
-        out[rows + rank * extra : rows + (rank + 1) * extra, :] = parts[rank, rows:, :]
-
-
-def aggregate_part(parts, rows):
-    shape = (2 * rows, parts.shape[2])
-    return pl.pallas_call(
-        aggregate_kernel,
-        out_shape=shape_of(shape),
-        in_specs=[VMEM],
-        out_specs=VMEM,
-        compiler_params=params(),
-        cost_estimate=cost(parts.size, parts.size * 2 + math.prod(shape) * 2),
-        name="aggregate_part",
-    )(parts)
-
-
-def layer_kernel(ranks, pos, pair, weight, mine, other, act, out, act_all, dz_all, term):
-    rows = pair.shape[1] // 2
-    width = pair.shape[2]
-    own = act.shape[0]
-    both = 2 * own
-    for rank in range(ranks):
-        span = slice(rank * both, (rank + 1) * both)
-        z_value = jnp.dot(pair[0, span, :], weight[:width, :], preferred_element_type=F32)
-        z_value += jnp.dot(pair[1, span, :], weight[width:, :], preferred_element_type=F32)
-        start = rows + rank * both
-        cot = jnp.concatenate(
-            [
-                jnp.concatenate(
-                    [pair[core, start + side * own : start + (side + 1) * own, :] for side in (0, 1)],
-                    axis=1,
-                )
-                for core in (0, 1)
-            ],
-            axis=0,
-        ).astype(F32)
-        sigma = jax.nn.sigmoid(z_value)
-        act_all[span, :] = (z_value * sigma).astype(BF16)
-        dz_all[span, :] = (cot * sigma * (1.0 + z_value * (1.0 - sigma))).astype(BF16)
-    x_index, core = pos[2], pos[3]
-    act[...] = act_all[pl.ds(pl.multiple_of((2 * x_index + core) * own, own), own), :]
-    dz_value = dz_all[...]
-    contract_rows = (((0,), (0,)), ((), ()))
-    contract_cols = (((1,), (1,)), ((), ()))
-    term[...] = lax.dot_general(
-        pair[core, :rows, :], dz_value, contract_rows, preferred_element_type=F32
-    )
-    weight_rows = weight[pl.ds(pl.multiple_of(core * width, width), width), :]
-    dy_turned = lax.dot_general(
-        weight_rows, dz_value, contract_cols, preferred_element_type=F32
+    )(pos, mine, other, blocks)
+
+
+def layer_kernel(parts, cot, weight, act, out):
+    replicas, own, width = parts.shape
+    ranks = replicas // 2
+    sides = []
+    for core in (0, 1):
+        side = parts[core].astype(F32)
+        for rank in range(1, ranks):
+            side += parts[2 * rank + core].astype(F32)
+        sides.append(side)
+    agg = jnp.concatenate(sides, axis=1).astype(BF16)
+    z_value = jnp.dot(agg, weight[...], preferred_element_type=F32)
+    sigma = jax.nn.sigmoid(z_value)
+    act[...] = (z_value * sigma).astype(BF16)
+    slope = cot[...].astype(F32) * sigma * (1.0 + z_value * (1.0 - sigma))
+    dz_value = slope.astype(BF16)
+    dy_value = lax.dot_general(
+        dz_value, weight[...], (((1,), (1,)), ((), ())), preferred_element_type=F32
+    ).astype(BF16)
+    term = lax.dot_general(
+        agg, dz_value, (((0,), (0,)), ((), ())), preferred_element_type=F32
     ).astype(BF16)
     chunk = width // ranks
-    piece = term[pl.ds(pl.multiple_of(x_index * chunk, chunk), chunk), :].astype(BF16)
-    piece = jnp.concatenate([piece[:, :width], piece[:, width:]], axis=0)
+    for rank in range(ranks):
+        for core in (0, 1):
+            target = 2 * rank + core
+            row = core * width + rank * chunk
+            out[target, :own, :] = dy_value[:, core * width : (core + 1) * width]
+            out[target, own : own + chunk, :] = term[row : row + chunk, :width]
+            out[target, own + chunk :, :] = term[row : row + chunk, width:]
+
+
+def layer_part(parts, cot, weight):
+    replicas, own, width = parts.shape
+    out = (replicas, own + 4 * width // replicas, width)
+    return pl.pallas_call(
+        layer_kernel,
+        out_shape=(shape_of(cot.shape), shape_of(out)),
+        in_specs=[VMEM] * 3,
+        out_specs=(VMEM, VMEM),
+        compiler_params=params(),
+        cost_estimate=cost(6 * own * 4 * width * width, math.prod(out) * 4),
+        name="layer_part",
+    )(parts, cot, weight)
+
+
+def backward_kernel(own, pos, parts, mine, other, out, held, sem):
+    copy = fetch(other, held, sem)
+    copy.start()
+    replicas, _, width = parts.shape
+    rows = replicas * own
+    piece = parts[0, own:, :].astype(F32)
+    for source in range(1, replicas):
+        piece += parts[source, own:, :].astype(F32)
+    piece = piece.astype(BF16)
     sections = out.shape[0]
-    for is_own, matrices in ((True, mine), (False, other)):
+    for target in range(sections):
+        out[target, rows:, :] = piece
+    dy_turned = parts[:, :own, :].reshape(rows, width).T
+    for is_own, matrices in ((True, mine), (False, held)):
+        if not is_own:
+            copy.wait()
         for section in range(sections // 2):
             grads = jnp.dot(dy_turned, matrices[section], preferred_element_type=F32)
             target = block_order(pos, sections, is_own, section)
             out[target, :rows, :] = grads.astype(BF16).T
-    for target in range(sections):
-        out[target, rows:, :] = piece
-
-
-def layer_part(pos, pair, weight, mine, other, ranks):
-    rows, width = pair.shape[1] // 2, pair.shape[2]
+
+
+def backward_part(pos, parts, mine, other, own):
+    replicas, height, width = parts.shape
+    rows = replicas * own
     sections = 2 * mine.shape[0]
-    own = rows // (2 * ranks)
-    out = (sections, rows + 2 * width // ranks, width)
+    out = (sections, rows + height - own, width)
 
     def kernel(*refs):
-        layer_kernel(ranks, *refs)
+        backward_kernel(own, *refs)
 
     return pl.pallas_call(
         kernel,
-        out_shape=(shape_of((own, 2 * width)), shape_of(out)),
-        in_specs=[SMEM] + [VMEM] * 4,
-        out_specs=(VMEM, VMEM),
-        scratch_shapes=[
-            pltpu.VMEM((rows, 2 * width), BF16),
-            pltpu.VMEM((rows, 2 * width), BF16),
-            pltpu.VMEM((width, 2 * width), F32),
-        ],
+        out_shape=shape_of(out),
+        in_specs=[SMEM, VMEM, VMEM, ANY],
+        out_specs=VMEM,
+        scratch_shapes=[pltpu.VMEM(other.shape, BF16), pltpu.SemaphoreType.DMA],
         compiler_params=params(),
         cost_estimate=cost(
             2 * sections * rows * rows * width, mine.size * 4 + math.prod(out) * 2
         ),
-        name="layer_part",
-    )(pos, pair, weight, mine, other)
+        name="backward_part",
+    )(pos, parts, mine, other)
 
 
 def planes_kernel(rows, pos, parts, out):
@@ -393,16 +356,18 @@
     mine = dense_blocks(tile_values[0], tile_rows[0], tile_cols[0], tile_count[0], rows)
     other = lax.ppermute(mine, "core", [(0, 1), (1, 0)])
 
-    half = lax.dynamic_slice_in_dim(features, core * width, width, axis=1)
-    planes = lax.all_gather(half, "z", axis=0, tiled=False)
-    blocks = exchange(window_pieces(pos, planes, sections), "y")
-    part = forward_part(pos, mine, other, blocks, cotangent)
-    parts = lax.all_gather(part, "x", axis=0, tiled=False)
-    pair = lax.all_gather(aggregate_part(parts, rows), "core", axis=0, tiled=False)
-    activations, pieces = layer_part(pos, pair, weight, mine, other, ranks)
-    pieces = exchange(pieces, "y")
+    share = rows // ranks
+    corner = (lax.axis_index("x") * share, core * width)
+    piece = lax.dynamic_slice(features, corner, (share, width))
+    planes = exchange(jnp.broadcast_to(piece, (depth, share, width)), "z")
+    blocks = exchange(window_pieces(pos, planes, sections, ranks), ("y", "x"))
+    part = forward_part(pos, mine, other, blocks.reshape(sections, rows, width))
+    parts = exchange(part.reshape(2 * ranks, own, width), ("x", "core"))
+    activations, pieces = layer_part(parts, cotangent, weight)
+    parts = exchange(pieces, ("x", "core"))
+    pieces = exchange(backward_part(pos, parts, mine, other, own), "y")
     pieces = exchange(planes_part(pos, pieces, rows, ranks), "x")
-    pieces = exchange(depth_part(pos, pieces, rows // ranks, depth), "z")
+    pieces = exchange(depth_part(pos, pieces, share, depth), "z")
     pair = lax.all_gather(total_part(pieces), "core", axis=0, tiled=False)
     weight_grad, feature_grad = finish_part(pos, pair, ranks, own, nodes)
     return (activations, weight_grad, feature_grad)

time: 244 us -> 190 us (0.78)
  waiting for transfers between devices: 96.3 us -> 25.8 us
  blocking collectives: 87.7 us -> 111 us
  between operations: 14.1 us -> 0.72 us
  starting transfers between devices: 22.8 us -> 33.3 us
  local copies, waits for them, and re-layouts: 8.46 us -> 4.83 us
    all_gather x2 -> x0, waiting for transfers between devices: 71.2 us -> none  [the longest x1 36.6 us: per_device(): parts = lax.all_gather(part, 'x', axis=0, tiled=False)]
    all_to_all x3 -> x5, blocking collectives: 74.4 us -> 107 us  [exchange(): return lax.all_to_all(pieces, axis, split_axis=0, concat_axis=0, tiled=True)]
    all_to_all x1 -> x2, starting transfers between devices: 6.68 us -> 30.4 us  [exchange(): return lax.all_to_all(pieces, axis, split_axis=0, concat_axis=0, tiled=True)]
    ppermute x1, starting transfers between devices: 16.1 us -> 2.91 us  [per_device(): other = lax.ppermute(mine, 'core', [(0, 1), (1, 0)])]
    all_gather x1 -> x0, blocking collectives: 6.66 us -> none  [per_device(): lax.all_gather(aggregate_part(parts, rows), 'core', axis=0, tiled=False)]
    unnamed x20 -> x12, local copies, waits for them, and re-layouts: 7.79 us -> 3.43 us
    all_gather x1, blocking collectives: 6.57 us -> 3.84 us  [per_device(): pair = lax.all_gather(total_part(pieces), 'core', axis=0, tiled=False)]
    all_to_all x1 -> x2, waiting for transfers between devices: 25.1 us -> 25.8 us  [exchange(): return lax.all_to_all(pieces, axis, split_axis=0, concat_axis=0, tiled=True)]
  transfers between devices with their start and end apart: 4 -> 3, of which waited for: 3 -> 1; matrix products, arithmetic and copies ran while one was open for 0% -> 0% of each run, Pallas kernels for 1% -> 2%
where the time goes in v2:
time: 190 us
  blocking collectives  111 us (58%)
  starting transfers between devices  33.3 us (18%)
  waiting for transfers between devices  25.8 us (14%)
  Pallas kernels  13.8 us (7%)
  local copies, waits for them, and re-layouts  4.83 us (3%)
    all_to_all x5, blocking collectives, exchange(): return lax.all_to_all(pieces, axis, split_axis=0, concat_axis=0, tiled=True)  107 us
    all_to_all x2, starting transfers between devices, exchange(): return lax.all_to_all(pieces, axis, split_axis=0, concat_axis=0, tiled=True)  30.4 us
    all_to_all x2, waiting for transfers between devices, exchange(): return lax.all_to_all(pieces, axis, split_axis=0, concat_axis=0, tiled=True)  25.8 us
    pallas_call x1, Pallas kernels, forward_part(): pl.pallas_call(forward_kernel, out_shape=shape_of((rows, width)), in_spec...  4.4 us
    all_gather x1, blocking collectives, per_device(): pair = lax.all_gather(total_part(pieces), 'core', axis=0, tiled=False)  3.84 us
  transfers between devices with their start and end apart: 3, of which 1 were waited for; matrix products, arithmetic and copies ran while one was open for 0% of the time, Pallas kernels for 2%

profile of v2, /device:TPU:1, one launch (start us, length us, event | category | flops | bytes accessed | tf_op | source)
XLA Modules:
  0.0 189.6 jit_solution(9316592407996907790)
XLA Ops:
  0.6 0.7 dynamic_slice.3
  1.4 0.7 broadcast_in_dim.3
  2.0 17.2 %all-to-all-start = ((bf16[8,64,128]{2,1,0:T(8,128)(2,1)}), bf16[8,64,128]{2,1,0:T(8,128)(2,1)S(1)}, u32[]{:S(2)}, u32[]{:S(2)}) async-start(bf16[8,64,128]{2,1,0:T(8,128)(2,1)} %broadcast_in_dim.3), calls=%async_computation | async-start | bytes 262144 | tf_op jit(solution)/shard_map/all_to_all | solution.py:342
  19.3 0.0 copy-start
  19.3 1.4 copy-done
  20.7 0.0 copy-start.3
  20.7 0.7 copy-done.3
  21.4 0.0 copy-start.4
  21.4 0.7 copy-done.4
  22.0 0.0 copy-start.5
  22.0 0.7 copy-done.5
  22.7 1.4 dense_blocks.1.mine.refs_2_
  24.1 2.9 %collective-permute-start = (bf16[4,512,512]{2,1,0:T(8,128)(2,1)S(1)}, bf16[4,512,512]{2,1,0:T(8,128)(2,1)}, u32[]{:S(2)}, u32[]{:S(2)}) collective-permute-start(bf16[4,512,512]{2,1,0:T(8,128)(2,1)S(1)} %dense_blocks.1.mine.refs_2_), channel_id=1, source_target_pairs={{0,1},{1,0},{2,3},{3,2},{4,5},{5,4},{6,7},{7,6},{8,9},{9,8},{10,11... | collective-permute-start | bytes 6291464 | tf_op jit(solution)/shard_map/ppermute | solution.py:357
  27.0 0.1 pad_add_fusion.pos.refs_0_
  27.1 0.0 all-to-all-done.planes
  27.1 1.7 window_pieces.1
  28.8 13.2 %all-to-all-start.1 = ((bf16[64,64,128]{2,1,0:T(8,128)(2,1)}), bf16[64,64,128]{2,1,0:T(8,128)(2,1)S(1)}, u32[]{:S(2)}, u32[]{:S(2)}) async-start(bf16[64,64,128]{2,1,0:T(8,128)(2,1)} %window_pieces.1), calls=%async_computation.1 | async-start | bytes 2097152 | tf_op jit(solution)/shard_map/all_to_all | solution.py:342
  42.0 0.0 collective-permute-done.other.refs_3_
  42.0 25.8 %all-to-all-done.1 = bf16[64,64,128]{2,1,0:T(8,128)(2,1)S(1)} async-done(((bf16[64,64,128]{2,1,0:T(8,128)(2,1)}), bf16[64,64,128]{2,1,0:T(8,128)(2,1)S(1)}, u32[]{:S(2)}, u32[]{:S(2)}) %all-to-all-start.1) | async-done | bytes 1048608 | tf_op jit(solution)/shard_map/all_to_all | solution.py:342
  67.8 0.0 copy-start.1
  67.8 0.0 copy-start.2
  67.8 4.4 %forward_part.1 = bf16[512,128]{1,0:T(8,128)(2,1)S(1)} custom-call(s32[4]{0:T(128)S(1)} %pad_add_fusion.pos.refs_0_, bf16[4,512,512]{2,1,0:T(8,128)(2,1)S(1)} %dense_blocks.1.mine.refs_2_, bf16[4,512,512]{2,1,0:T(8,128)(2,1)} %collective-permute-done.other.refs_3_, bf16[8,512,128]{2,1,0:T(8,128)(2,1)S(1)} %bitcast.11), custom_call_target="tpu_custom_call" | custom-call | flops 536870912 | bytes 5242880 | tf_op jit(solution)/shard_map/forward_part/pallas_call | solution.py:111
  72.2 18.6 %all_to_all.35.parts = bf16[16,32,128]{2,1,0:T(8,128)(2,1)S(1)} all-to-all(bf16[16,32,128]{2,1,0:T(8,128)(2,1)S(1)} %bitcast.14), channel_id=1, replica_groups=mesh['z'=8,'y'=8,'x'=8,'core'=2] {'x','core'}, dimensions={0} | all-to-all | bytes 262144 | tf_op jit(solution)/shard_map/all_to_all | solution.py:342
  90.7 0.0 copy-done.1
  90.7 0.0 copy-done.2
  90.7 0.8 layer_part.1
  91.5 14.1 %all_to_all.36.refs_1_ = bf16[16,64,128]{2,1,0:T(8,128)(2,1)S(1)} all-to-all(bf16[16,64,128]{2,1,0:T(8,128)(2,1)S(1)} %get-tuple-element.8), channel_id=1, replica_groups=mesh['z'=8,'y'=8,'x'=8,'core'=2] {'x','core'}, dimensions={0} | all-to-all | bytes 524288 | tf_op jit(solution)/shard_map/all_to_all | solution.py:342
  105.6 2.7 %backward_part.1 = bf16[8,544,128]{2,1,0:T(8,128)(2,1)S(1)} custom-call(s32[4]{0:T(128)S(1)} %pad_add_fusion.pos.refs_0_, bf16[16,64,128]{2,1,0:T(8,128)(2,1)S(1)} %all_to_all.36.refs_1_, bf16[4,512,512]{2,1,0:T(8,128)(2,1)S(1)} %dense_blocks.1.mine.refs_2_, bf16[4,512,512]{2,1,0:T(8,128)(2,1)} %collective-permute-done.other.refs_3_), custom_call_target="tpu_custom_call" | custom-call | flops 536870912 | bytes 5308416 | tf_op jit(solution)/shard_map/backward_part/pallas_call | solution.py:201
  108.3 33.1 %all_to_all.37.refs_1_ = bf16[8,544,128]{2,1,0:T(8,128)(2,1)S(1)} all-to-all(bf16[8,544,128]{2,1,0:T(8,128)(2,1)S(1)} %backward_part.1), channel_id=1, replica_groups=mesh['z'=8,'y'=8,'x'=8,'core'=2] {'y'}, dimensions={0} | all-to-all | bytes 2228224 | tf_op jit(solution)/shard_map/all_to_all | solution.py:342
  141.4 0.9 planes_part.1
  142.3 15.5 %all_to_all.38.refs_1_ = bf16[8,160,128]{2,1,0:T(8,128)(2,1)S(1)} all-to-all(bf16[8,160,128]{2,1,0:T(8,128)(2,1)S(1)} %planes_part.1), channel_id=1, replica_groups=mesh['z'=8,'y'=8,'x'=8,'core'=2] {'x'}, dimensions={0} | all-to-all | bytes 655360 | tf_op jit(solution)/shard_map/all_to_all | solution.py:342
  157.9 0.6 depth_part.1
  158.5 25.9 %all_to_all.39.parts = bf16[8,320,128]{2,1,0:T(8,128)(2,1)S(1)} all-to-all(bf16[8,320,128]{2,1,0:T(8,128)(2,1)S(1)} %depth_part.1), channel_id=1, replica_groups=mesh['z'=8,'y'=8,'x'=8,'core'=2] {'z'}, dimensions={0} | all-to-all | bytes 1310720 | tf_op jit(solution)/shard_map/all_to_all | solution.py:342
  184.4 0.1 total_part.1
  184.5 3.8 %all-gather = bf16[640,128]{1,0:T(8,128)(2,1)S(1)} all-gather(bf16[320,128]{1,0:T(8,128)(2,1)S(1)} %total_part.1), channel_id=2, replica_groups=mesh['z'=8,'y'=8,'x'=8,'core'=2] {'core'}, dimensions={0}, use_global_device_ids=true | all-gather | bytes 245760 | tf_op jit(solution)/shard_map/all_gather | solution.py:371
  188.4 1.3 finish_part.1
Async XLA Ops:
  2.0 25.1 %all-to-all-start = ((bf16[8,64,128]{2,1,0:T(8,128)(2,1)}), bf16[8,64,128]{2,1,0:T(8,128)(2,1)S(1)}, u32[]{:S(2)}, u32[]{:S(2)}) async-start(bf16[8,64,128]{2,1,0:T(8,128)(2,1)} %broadcast_in_dim.3), calls=%async_computation | async-start | bytes 262144 | tf_op jit(solution)/shard_map/all_to_all | solution.py:342
  19.3 1.4 copy-start
  20.7 0.7 copy-start.3
  21.4 0.7 copy-start.4
  22.0 0.7 copy-start.5
  24.1 17.9 %collective-permute-start = (bf16[4,512,512]{2,1,0:T(8,128)(2,1)S(1)}, bf16[4,512,512]{2,1,0:T(8,128)(2,1)}, u32[]{:S(2)}, u32[]{:S(2)}) collective-permute-start(bf16[4,512,512]{2,1,0:T(8,128)(2,1)S(1)} %dense_blocks.1.mine.refs_2_), channel_id=1, source_target_pairs={{0,1},{1,0},{2,3},{3,2},{4,5},{5,4},{6,7},{7,6},{8,9},{9,8},{10,11... | collective-permute-start | bytes 6291464 | tf_op jit(solution)/shard_map/ppermute | solution.py:357
  28.8 39.0 %all-to-all-start.1 = ((bf16[64,64,128]{2,1,0:T(8,128)(2,1)}), bf16[64,64,128]{2,1,0:T(8,128)(2,1)S(1)}, u32[]{:S(2)}, u32[]{:S(2)}) async-start(bf16[64,64,128]{2,1,0:T(8,128)(2,1)} %window_pieces.1), calls=%async_computation.1 | async-start | bytes 2097152 | tf_op jit(solution)/shard_map/all_to_all | solution.py:342
  67.8 23.0 %copy-start.1 = (bf16[256,256]{1,0:T(8,128)(2,1)S(1)}, bf16[256,256]{1,0:T(8,128)(2,1)}, u32[]{:S(2)}) copy-start(bf16[256,256]{1,0:T(8,128)(2,1)} %weight.1) | copy-start | bytes 393220
  67.8 23.0 %copy-start.2 = (bf16[32,256]{1,0:T(8,128)(2,1)S(1)}, bf16[32,256]{1,0:T(8,128)(2,1)}, u32[]{:S(2)}) copy-start(bf16[32,256]{1,0:T(8,128)(2,1)} %cot.1) | copy-start | bytes 49156

commit v3 on v2

v3 whole, which is shorter than its diff:
```python
import math

import jax
import jax.numpy as jnp
from jax import lax
from jax.experimental import pallas as pl
from jax.experimental.pallas import tpu as pltpu
from jax.sharding import Mesh
from jax.sharding import PartitionSpec as P

TILE = 128
BF16 = jnp.bfloat16
F32 = jnp.float32
VMEM = pl.BlockSpec(memory_space=pltpu.VMEM)
SMEM = pl.BlockSpec(memory_space=pltpu.SMEM)
ANY = pl.BlockSpec(memory_space=pl.ANY)


def params(mib=40):
    return pltpu.CompilerParams(vmem_limit_bytes=mib << 20)


def shape_of(shape, dtype=BF16):
    return jax.ShapeDtypeStruct(shape, dtype)


def cost(flops, nbytes):
    return pl.CostEstimate(flops=flops, bytes_accessed=nbytes, transcendentals=0)


def dense_kernel(rows, cols, count, tiles, out):
    section = pl.program_id(0)
    out[...] = jnp.zeros_like(out)
    for slot in range(tiles.shape[1]):

        @pl.when(slot < count[section])
        def _():
            row = pl.multiple_of(rows[section, slot] * TILE, TILE)
            col = pl.multiple_of(cols[section, slot] * TILE, TILE)
            out[pl.ds(row, TILE), pl.ds(col, TILE)] = tiles[0, slot]


def dense_blocks(tiles, rows, cols, count, rows_blk):
    sections, slots = tiles.shape[:2]
    return pl.pallas_call(
        dense_kernel,
        grid=(sections,),
        out_shape=shape_of((rows_blk, sections * rows_blk)),
        in_specs=[
            SMEM,
            SMEM,
            SMEM,
            pl.BlockSpec((1, slots, TILE, TILE), lambda i: (i, 0, 0, 0)),
        ],
        out_specs=pl.BlockSpec((rows_blk, rows_blk), lambda i: (0, i)),
        compiler_params=params(),
        cost_estimate=cost(0, tiles.size * 2 + sections * rows_blk * rows_blk * 2),
        name="dense_blocks",
    )(rows, cols, count, tiles)


def light_kernel(pos, planes, out):
    ranks, share = planes.shape[:2]
    first = pos[0] + pos[2]
    for target in range(ranks):
        ahead = ((target > pos[1]) & (pos[3] == 1)).astype(jnp.int32)
        out[target, :share, :] = planes[lax.rem(first + ahead, ranks)]
        out[target, share:, :] = planes[lax.rem(first + 1, ranks)]


def light_pieces(pos, planes):
    ranks, share, width = planes.shape
    shape = (ranks, 2 * share, width)
    return pl.pallas_call(
        light_kernel,
        out_shape=shape_of(shape),
        in_specs=[SMEM, VMEM],
        out_specs=VMEM,
        compiler_params=params(),
        cost_estimate=cost(0, math.prod(shape) * 2),
        name="light_pieces",
    )(pos, planes)


def heavy_kernel(pos, parts, out):
    ranks = parts.shape[0]
    share = parts.shape[1] // 2
    for target in range(ranks):
        ahead = ((target > pos[1]) & (pos[3] == 0)).astype(jnp.int32)
        start = pl.multiple_of(ahead * share, share)
        for rank in range(ranks):
            out[target, rank] = parts[rank, pl.ds(start, share), :]


def heavy_pieces(pos, parts):
    ranks, height, width = parts.shape
    shape = (ranks, ranks, height // 2, width)
    return pl.pallas_call(
        heavy_kernel,
        out_shape=shape_of(shape),
        in_specs=[SMEM, VMEM],
        out_specs=VMEM,
        compiler_params=params(),
        cost_estimate=cost(0, math.prod(shape) * 2),
        name="heavy_pieces",
    )(pos, parts)


def block_order(pos, sections, own, section):
    core = pos[3] if own else 1 - pos[3]
    return lax.rem(pos[1] + core * (sections // 2) + section, sections)


def forward_kernel(pos, mine, other, parts, out, held, sem):
    copy = pltpu.make_async_copy(other, held, sem)
    copy.start()
    ranks = parts.shape[0]
    flip = pos[3]
    turned = None
    for is_own, matrix in ((True, mine), (False, held)):
        slices = []
        for section in range(ranks // 2):
            block = block_order(pos, ranks, is_own, section)
            for rank in range(ranks):
                outer = jnp.where(flip == 0, block, rank)
                inner = jnp.where(flip == 0, rank, block)
                slices.append(parts[outer, inner])
        if not is_own:
            copy.wait()
        product = lax.dot_general(
            jnp.concatenate(slices, axis=0).T,
            matrix[...],
            (((1,), (1,)), ((), ())),
            preferred_element_type=F32,
        )
        turned = product if turned is None else turned + product
    out[...] = turned.astype(BF16).T


def forward_part(pos, mine, other, parts):
    rows, columns = mine.shape
    width = parts.shape[-1]
    return pl.pallas_call(
        forward_kernel,
        out_shape=shape_of((rows, width)),
        in_specs=[SMEM, VMEM, ANY, VMEM],
        out_specs=VMEM,
        scratch_shapes=[pltpu.VMEM(other.shape, BF16), pltpu.SemaphoreType.DMA],
        compiler_params=params(),
        cost_estimate=cost(4 * rows * columns * width, 4 * rows * columns + parts.size * 2),
        name="forward_part",
    )(pos, mine, other, parts)


def layer_kernel(pos, parts, cot, weight, act, out, term):
    replicas, own, width = parts.shape
    ranks = replicas // 2
    sides = []
    for core in (0, 1):
        side = parts[core].astype(F32)
        for rank in range(1, ranks):
            side += parts[2 * rank + core].astype(F32)
        sides.append(side)
    agg = jnp.concatenate(sides, axis=1).astype(BF16)
    z_value = jnp.dot(agg, weight[...], preferred_element_type=F32)
    sigma = jax.nn.sigmoid(z_value)
    act[...] = (z_value * sigma).astype(BF16)
    slope = cot[...].astype(F32) * sigma * (1.0 + z_value * (1.0 - sigma))
    dz_value = slope.astype(BF16)
    dy_value = lax.dot_general(
        dz_value, weight[...], (((1,), (1,)), ((), ())), preferred_element_type=F32
    ).astype(BF16)
    term[...] = lax.dot_general(
        agg, dz_value, (((0,), (0,)), ((), ())), preferred_element_type=F32
    ).astype(BF16)
    chunk = width // ranks
    for rank in range(ranks):
        for core in (0, 1):
            target = 2 * rank + core
            row = core * width + lax.rem(pos[0] + rank, ranks) * chunk
            piece = term[pl.ds(pl.multiple_of(row, chunk), chunk), :]
            out[target, :own, :] = dy_value[:, core * width : (core + 1) * width]
            out[target, own : own + chunk, :] = piece[:, :width]
            out[target, own + chunk :, :] = piece[:, width:]


def layer_part(pos, parts, cot, weight):
    replicas, own, width = parts.shape
    out = (replicas, own + 4 * width // replicas, width)
    return pl.pallas_call(
        layer_kernel,
        out_shape=(shape_of(cot.shape), shape_of(out)),
        in_specs=[SMEM, VMEM, VMEM, VMEM],
        out_specs=(VMEM, VMEM),
        scratch_shapes=[pltpu.VMEM(weight.shape, BF16)],
        compiler_params=params(),
        cost_estimate=cost(6 * own * 4 * width * width, math.prod(out) * 4),
        name="layer_part",
    )(pos, parts, cot, weight)


def backward_kernel(own, pos, parts, mine, other, out, held, sem):
    copy = pltpu.make_async_copy(other, held, sem)
    copy.start()
    replicas, _, width = parts.shape
    ranks = replicas // 2
    rows = replicas * own
    share = rows // ranks
    piece = parts[0, own:, :].astype(F32)
    for source in range(1, replicas):
        piece += parts[source, own:, :].astype(F32)
    piece = piece.astype(BF16)
    for target in range(ranks):
        out[target, rows:, :] = piece
    dy_turned = parts[:, :own, :].reshape(rows, width).T
    flip = pos[3]
    for is_own, matrix in ((True, mine), (False, held)):
        if not is_own:
            copy.wait()
        for section in range(ranks // 2):
            side = matrix[:, section * rows : (section + 1) * rows]
            grads = jnp.dot(dy_turned, side, preferred_element_type=F32).astype(BF16).T
            block = block_order(pos, ranks, is_own, section)
            for rank in range(ranks):
                outer = jnp.where(flip == 0, block, rank)
                inner = jnp.where(flip == 0, rank, block)
                start = pl.multiple_of(inner * share, share)
                out[outer, pl.ds(start, share), :] = grads[rank * share : (rank + 1) * share, :]


def backward_part(pos, parts, mine, other, own):
    replicas, height, width = parts.shape
    rows, columns = mine.shape
    out = (replicas // 2, rows + height - own, width)

    def kernel(*refs):
        backward_kernel(own, *refs)

    return pl.pallas_call(
        kernel,
        out_shape=shape_of(out),
        in_specs=[SMEM, VMEM, VMEM, ANY],
        out_specs=VMEM,
        scratch_shapes=[pltpu.VMEM(other.shape, BF16), pltpu.SemaphoreType.DMA],
        compiler_params=params(),
        cost_estimate=cost(4 * rows * columns * width, 4 * rows * columns + math.prod(out) * 2),
        name="backward_part",
    )(pos, parts, mine, other)


def merge_kernel(rows, pos, parts, out):
    ranks, height, width = parts.shape
    share = rows // ranks
    term = parts[0, rows:, :].astype(F32)
    for source in range(1, ranks):
        term += parts[source, rows:, :].astype(F32)
    term = term.astype(BF16)
    for target in range(ranks):
        near = jnp.zeros((share, width), F32)
        far = near
        for source in range(ranks):
            value = parts[source, target * share : (target + 1) * share, :].astype(F32)
            same = (source <= pos[1]) | (pos[3] == 1)
            near += jnp.where(same, value, 0.0)
            far += jnp.where(same, 0.0, value)
        out[target, :share, :] = near.astype(BF16)
        out[target, share : 2 * share, :] = far.astype(BF16)
        out[target, 2 * share :, :] = term


def merge_part(pos, parts, rows):
    ranks, height, width = parts.shape
    shape = (ranks, 2 * rows // ranks + height - rows, width)

    def kernel(*refs):
        merge_kernel(rows, *refs)

    return pl.pallas_call(
        kernel,
        out_shape=shape_of(shape),
        in_specs=[SMEM, VMEM],
        out_specs=VMEM,
        compiler_params=params(),
        cost_estimate=cost(parts.size * 2, parts.size * 2 + math.prod(shape) * 2),
        name="merge_part",
    )(pos, parts)


def place_kernel(share, pos, parts, out):
    ranks, height, width = parts.shape
    own = share // 2
    near = jnp.zeros((share, width), F32)
    far = near
    term = jnp.zeros((height - 2 * share, width), F32)
    for source in range(ranks):
        first = parts[source, :share, :].astype(F32)
        second = parts[source, share : 2 * share, :].astype(F32)
        same = (source <= pos[1]) | (pos[3] == 0)
        near += jnp.where(same, first, 0.0)
        far += jnp.where(same, second, first)
        term += parts[source, 2 * share :, :].astype(F32)
    near, far, term = near.astype(BF16), far.astype(BF16), term.astype(BF16)
    plane = lax.rem(pos[0] + pos[2], ranks)
    behind = lax.rem(pos[0] + pos[2] + 1, ranks)
    nothing = jnp.zeros_like(near)
    for target in range(ranks):
        value = jnp.where(plane == target, near, jnp.where(behind == target, far, nothing))
        for core in (0, 1):
            out[2 * target + core, :own, :] = value[core * own : (core + 1) * own, :]
            out[2 * target + core, own:, :] = term


def place_part(pos, parts, share):
    ranks, height, width = parts.shape
    shape = (2 * ranks, height - 3 * share // 2, width)

    def kernel(*refs):
        place_kernel(share, *refs)

    return pl.pallas_call(
        kernel,
        out_shape=shape_of(shape),
        in_specs=[SMEM, VMEM],
        out_specs=VMEM,
        compiler_params=params(),
        cost_estimate=cost(parts.size, parts.size * 2 + math.prod(shape) * 2),
        name="place_part",
    )(pos, parts)


def finish_kernel(scale, pos, parts, term, grads):
    replicas, height, width = parts.shape
    ranks = replicas // 2
    own = grads.shape[0]
    chunk = width // ranks
    for core in (0, 1):
        total = parts[core, :own, :].astype(F32)
        for depth in range(1, ranks):
            total += parts[2 * depth + core, :own, :].astype(F32)
        grads[:, core * width : (core + 1) * width] = total.astype(BF16)
        for depth in range(ranks):
            row = core * width + lax.rem(pos[2] + depth, ranks) * chunk
            for side in (0, 1):
                first = own + side * chunk
                value = parts[2 * depth + core, first : first + chunk, :].astype(F32) / scale
                term[pl.ds(pl.multiple_of(row, chunk), chunk), side * width : (side + 1) * width] = value


def finish_part(pos, parts, own, nodes):
    width = parts.shape[2]

    def kernel(*refs):
        finish_kernel(math.sqrt(nodes), *refs)

    return pl.pallas_call(
        kernel,
        out_shape=(shape_of((2 * width, 2 * width), F32), shape_of((own, 2 * width))),
        in_specs=[SMEM, VMEM],
        out_specs=(VMEM, VMEM),
        compiler_params=params(),
        cost_estimate=cost(parts.size, parts.size * 2),
        name="finish_part",
    )(pos, parts)


def device_at(ranks, depth, section, rank, core):
    return ((depth % ranks * ranks + section) * ranks + rank) * 2 + core


def groups(ranks, kinds):
    found = []
    for core, kind in enumerate(kinds):
        for a in range(ranks):
            for b in range(ranks):
                if kind == "line":
                    found.append([device_at(ranks, a, k, b, core) for k in range(ranks)])
                else:
                    found.append([device_at(ranks, a - k, b, k, core) for k in range(ranks)])
    return found


def grouped(pieces, ranks, kinds):
    return lax.all_to_all(
        pieces,
        ("z", "y", "x", "core"),
        split_axis=0,
        concat_axis=0,
        axis_index_groups=groups(ranks, kinds),
        tiled=True,
    )


def exchange(pieces, axis):
    return lax.all_to_all(pieces, axis, split_axis=0, concat_axis=0, tiled=True)


def per_device(features, weight, cotangent, tile_values, tile_rows, tile_cols, tile_count):
    rows, columns = features.shape
    width = columns // 2
    ranks = lax.axis_size("x")
    share = rows // ranks
    own = share // 2
    core = lax.axis_index("core")
    pos = jnp.stack(
        [lax.axis_index("z"), lax.axis_index("y"), lax.axis_index("x"), core]
    ).astype(jnp.int32)

    mine = dense_blocks(tile_values[0], tile_rows[0], tile_cols[0], tile_count[0], rows)
    other = lax.ppermute(mine, "core", [(0, 1), (1, 0)])

    corner = (lax.axis_index("x") * share, core * width)
    piece = lax.dynamic_slice(features, corner, (share, width))
    planes = exchange(jnp.broadcast_to(piece, (ranks, share, width)), "z")
    parts = grouped(light_pieces(pos, planes), ranks, ("diagonal", "line"))
    parts = grouped(heavy_pieces(pos, parts), ranks, ("line", "diagonal"))
    part = forward_part(pos, mine, other, parts)
    parts = exchange(part.reshape(2 * ranks, own, width), ("x", "core"))
    activations, pieces = layer_part(pos, parts, cotangent, weight)
    parts = exchange(pieces, ("x", "core"))
    pieces = backward_part(pos, parts, mine, other, own)
    parts = grouped(pieces, ranks, ("line", "diagonal"))
    parts = grouped(merge_part(pos, parts, rows), ranks, ("diagonal", "line"))
    parts = exchange(place_part(pos, parts, share), ("z", "core"))
    weight_grad, feature_grad = finish_part(pos, parts, own, rows * ranks * ranks)
    return (activations, weight_grad, feature_grad)


def solution(mesh):
    blk, rep = mesh.devices.shape
    ranks = rep // 2
    devices = mesh.devices.reshape(ranks, blk // ranks, ranks, 2)
    grid = Mesh(devices, ("z", "y", "x", "core"))
    blk_axes, rep_axes = ("z", "y"), ("x", "core")
    return jax.shard_map(
        per_device,
        mesh=grid,
        in_specs=(
            P(blk_axes, None),
            P(),
            P(blk_axes + rep_axes, None),
            P(blk_axes, rep_axes, None, None, None),
            P(blk_axes, rep_axes, None),
            P(blk_axes, rep_axes, None),
            P(blk_axes, rep_axes),
        ),
        out_specs=(P(blk_axes + rep_axes, None), P(), P(blk_axes + rep_axes, None)),
        check_vma=False,
    )
```

time: 190 us -> 184 us (0.968)
  blocking collectives: 111 us -> 91.9 us
  waiting for transfers between devices: 25.8 us -> 31.6 us
  starting transfers between devices: 33.3 us -> 38.8 us
  Pallas kernels: 13.8 us -> 15.8 us
    all_to_all x5 -> x3, blocking collectives: 107 us -> 46.5 us  [exchange(): return lax.all_to_all(pieces, axis, split_axis=0, concat_axis=0, tiled=True)]
    all_to_all x0 -> x2, blocking collectives: none -> 45.4 us  [grouped(): lax.all_to_all(pieces, ('z', 'y', 'x', 'core'), split_axis=0, concat_axis...]
    all_to_all x0 -> x2, waiting for transfers between devices: none -> 23.9 us  [grouped(): lax.all_to_all(pieces, ('z', 'y', 'x', 'core'), split_axis=0, concat_axis...]
    all_to_all x2 -> x1, waiting for transfers between devices: 25.8 us -> 7.69 us  [exchange(): return lax.all_to_all(pieces, axis, split_axis=0, concat_axis=0, tiled=True)]
    all_to_all x0 -> x2, starting transfers between devices: none -> 17.9 us  [grouped(): lax.all_to_all(pieces, ('z', 'y', 'x', 'core'), split_axis=0, concat_axis...]
    all_to_all x2 -> x1, starting transfers between devices: 30.4 us -> 17.2 us  [exchange(): return lax.all_to_all(pieces, axis, split_axis=0, concat_axis=0, tiled=True)]
    all_gather x1 -> x0, blocking collectives: 3.84 us -> none  [per_device(): pair = lax.all_gather(total_part(pieces), 'core', axis=0, tiled=False)]
  transfers between devices with their start and end apart: 3 -> 4, of which waited for: 1 -> 3; matrix products, arithmetic and copies ran while one was open for 0% -> 0% of each run, Pallas kernels for 2% -> 2%
where the time goes in v3:
time: 184 us
  blocking collectives  91.9 us (50%)
  starting transfers between devices  38.8 us (21%)
  waiting for transfers between devices  31.6 us (17%)
  Pallas kernels  15.8 us (9%)
  local copies, waits for them, and re-layouts  4.83 us (3%)
    all_to_all x3, blocking collectives, exchange(): return lax.all_to_all(pieces, axis, split_axis=0, concat_axis=0, tiled=True)  46.5 us
    all_to_all x2, blocking collectives, grouped(): lax.all_to_all(pieces, ('z', 'y', 'x', 'core'), split_axis=0, concat_axis...  45.4 us
    all_to_all x2, waiting for transfers between devices, grouped(): lax.all_to_all(pieces, ('z', 'y', 'x', 'core'), split_axis=0, concat_axis...  23.9 us
    all_to_all x2, starting transfers between devices, grouped(): lax.all_to_all(pieces, ('z', 'y', 'x', 'core'), split_axis=0, concat_axis...  17.9 us
    all_to_all x1, starting transfers between devices, exchange(): return lax.all_to_all(pieces, axis, split_axis=0, concat_axis=0, tiled=True)  17.2 us
    all_to_all x1, waiting for transfers between devices, exchange(): return lax.all_to_all(pieces, axis, split_axis=0, concat_axis=0, tiled=True)  7.69 us
    pallas_call x1, Pallas kernels, forward_part(): pl.pallas_call(forward_kernel, out_shape=shape_of((rows, width)), in_spec...  4 us
  transfers between devices with their start and end apart: 4, of which 3 were waited for; matrix products, arithmetic and copies ran while one was open for 0% of the time, Pallas kernels for 2%

profile of v3, /device:TPU:1, one launch (start us, length us, event | category | flops | bytes accessed | tf_op | source)
XLA Modules:
  0.0 183.7 jit_solution(9541281988887615691)
XLA Ops:
  0.6 0.7 dynamic_slice.3
  1.4 0.7 broadcast_in_dim.3
  2.0 17.2 %all-to-all-start = ((bf16[8,64,128]{2,1,0:T(8,128)(2,1)}), bf16[8,64,128]{2,1,0:T(8,128)(2,1)S(1)}, u32[]{:S(2)}, u32[]{:S(2)}) async-start(bf16[8,64,128]{2,1,0:T(8,128)(2,1)} %broadcast_in_dim.3), calls=%async_computation | async-start | bytes 262144 | tf_op jit(solution)/shard_map/all_to_all | solution.py:394
  19.3 0.1 pad_add_fusion.pos.refs_0_
  19.3 7.7 %all-to-all-done.planes = bf16[8,64,128]{2,1,0:T(8,128)(2,1)S(1)} async-done(((bf16[8,64,128]{2,1,0:T(8,128)(2,1)}), bf16[8,64,128]{2,1,0:T(8,128)(2,1)S(1)}, u32[]{:S(2)}, u32[]{:S(2)}) %all-to-all-start) | async-done | bytes 131104 | tf_op jit(solution)/shard_map/all_to_all | solution.py:394
  27.0 1.3 light_pieces.1
  28.3 7.3 %all-to-all-start.1 = ((bf16[8,128,128]{2,1,0:T(8,128)(2,1)}), bf16[8,128,128]{2,1,0:T(8,128)(2,1)S(1)}, u32[]{:S(2)}, u32[]{:S(2)}) async-start(bf16[8,128,128]{2,1,0:T(8,128)(2,1)} %light_pieces.1), calls=%async_computation.1 | async-start | bytes 524288 | tf_op jit(solution)/shard_map/all_to_all | solution.py:383
  35.6 0.0 copy-start
  35.6 1.4 copy-done
  37.0 0.0 copy-start.3
  37.0 0.7 copy-done.3
  37.7 0.0 copy-start.4
  37.7 0.7 copy-done.4
  38.4 0.0 copy-start.5
  38.4 0.7 copy-done.5
  39.0 1.6 dense_blocks.1.mine.refs_2_
  40.7 3.7 %collective-permute-start = (bf16[512,2048]{1,0:T(8,128)(2,1)S(1)}, bf16[512,2048]{1,0:T(8,128)(2,1)}, u32[]{:S(2)}, u32[]{:S(2)}) collective-permute-start(bf16[512,2048]{1,0:T(8,128)(2,1)S(1)} %dense_blocks.1.mine.refs_2_), channel_id=1, source_target_pairs={{0,1},{1,0},{2,3},{3,2},{4,5},{5,4},{6,7},{7,6},{8,9},{9,8},{10,11... | collective-permute-start | bytes 6291464 | tf_op jit(solution)/shard_map/ppermute | solution.py:409
  44.3 0.9 all-to-all-done.1.parts
  45.2 1.6 heavy_pieces.1
  46.8 10.6 %all-to-all-start.2 = ((bf16[8,8,64,128]{3,2,1,0:T(8,128)(2,1)}), bf16[8,8,64,128]{3,2,1,0:T(8,128)(2,1)S(1)}, u32[]{:S(2)}, u32[]{:S(2)}) async-start(bf16[8,8,64,128]{3,2,1,0:T(8,128)(2,1)} %heavy_pieces.1), calls=%async_computation.2 | async-start | bytes 2097152 | tf_op jit(solution)/shard_map/all_to_all | solution.py:383
  57.4 0.0 copy-start.1
  57.5 0.0 copy-start.2
  57.5 0.0 collective-permute-done.other.refs_3_
  57.5 23.0 %all-to-all-done.2.parts = bf16[8,8,64,128]{3,2,1,0:T(8,128)(2,1)S(1)} async-done(((bf16[8,8,64,128]{3,2,1,0:T(8,128)(2,1)}), bf16[8,8,64,128]{3,2,1,0:T(8,128)(2,1)S(1)}, u32[]{:S(2)}, u32[]{:S(2)}) %all-to-all-start.2) | async-done | bytes 1048608 | tf_op jit(solution)/shard_map/all_to_all | solution.py:383
  80.5 4.0 %forward_part.1 = bf16[512,128]{1,0:T(8,128)(2,1)S(1)} custom-call(s32[4]{0:T(128)S(1)} %pad_add_fusion.pos.refs_0_, bf16[512,2048]{1,0:T(8,128)(2,1)S(1)} %dense_blocks.1.mine.refs_2_, bf16[512,2048]{1,0:T(8,128)(2,1)} %collective-permute-done.other.refs_3_, bf16[8,8,64,128]{3,2,1,0:T(8,128)(2,1)S(1)} %all-to-all-done.2.parts), custom_call_target="tpu_custom_call" | custom-call | flops 536870912 | bytes 5242880 | tf_op jit(solution)/shard_map/forward_part/pallas_call | solution.py:143
  84.5 14.2 %all_to_all.40.parts = bf16[16,32,128]{2,1,0:T(8,128)(2,1)S(1)} all-to-all(bf16[16,32,128]{2,1,0:T(8,128)(2,1)S(1)} %bitcast.10), channel_id=1, replica_groups=mesh['z'=8,'y'=8,'x'=8,'core'=2] {'x','core'}, dimensions={0} | all-to-all | bytes 262144 | tf_op jit(solution)/shard_map/all_to_all | solution.py:394
  98.7 0.0 copy-done.1
  98.7 0.0 copy-done.2
  98.7 1.3 layer_part.1
  100.0 14.1 %all_to_all.41.refs_1_ = bf16[16,64,128]{2,1,0:T(8,128)(2,1)S(1)} all-to-all(bf16[16,64,128]{2,1,0:T(8,128)(2,1)S(1)} %get-tuple-element.8), channel_id=1, replica_groups=mesh['z'=8,'y'=8,'x'=8,'core'=2] {'x','core'}, dimensions={0} | all-to-all | bytes 524288 | tf_op jit(solution)/shard_map/all_to_all | solution.py:394
  114.1 3.1 %backward_part.1 = bf16[8,544,128]{2,1,0:T(8,128)(2,1)S(1)} custom-call(s32[4]{0:T(128)S(1)} %pad_add_fusion.pos.refs_0_, bf16[16,64,128]{2,1,0:T(8,128)(2,1)S(1)} %all_to_all.41.refs_1_, bf16[512,2048]{1,0:T(8,128)(2,1)S(1)} %dense_blocks.1.mine.refs_2_, bf16[512,2048]{1,0:T(8,128)(2,1)} %collective-permute-done.other.refs_3_), custom_call_target="tpu_custom_call" | custom-call | flops 536870912 | bytes 5308416 | tf_op jit(solution)/shard_map/backward_part/pallas_call | solution.py:239
  117.2 27.6 %all_to_all.42.refs_1_ = bf16[8,544,128]{2,1,0:T(8,128)(2,1)S(1)} all-to-all(bf16[8,544,128]{2,1,0:T(8,128)(2,1)S(1)} %backward_part.1), channel_id=1, replica_groups={{0,16,32,48,64,80,96,112},{2,18,34,50,66,82,98,114},{4,20,36,52,68,84,1..., dimensions={0} | all-to-all | bytes 2228224 | tf_op jit(solution)/shard_map/all_to_all | solution.py:383
  144.8 0.9 merge_part.1
  145.8 17.9 %all_to_all.43.refs_1_ = bf16[8,160,128]{2,1,0:T(8,128)(2,1)S(1)} all-to-all(bf16[8,160,128]{2,1,0:T(8,128)(2,1)S(1)} %merge_part.1), channel_id=1, replica_groups={{0,898,772,646,520,394,268,142},{16,914,788,662,536,410,284,158},{32,93..., dimensions={0} | all-to-all | bytes 655360 | tf_op jit(solution)/shard_map/all_to_all | solution.py:383
  163.6 0.6 place_part.1
  164.3 18.2 %all_to_all.44.refs_1_ = bf16[16,64,128]{2,1,0:T(8,128)(2,1)S(1)} all-to-all(bf16[16,64,128]{2,1,0:T(8,128)(2,1)S(1)} %place_part.1), channel_id=1, replica_groups=mesh['z'=8,'y'=8,'x'=8,'core'=2] {'z','core'}, dimensions={0} | all-to-all | bytes 524288 | tf_op jit(solution)/shard_map/all_to_all | solution.py:394
  182.4 1.3 finish_part.1
Async XLA Ops:
  2.0 25.0 %all-to-all-start = ((bf16[8,64,128]{2,1,0:T(8,128)(2,1)}), bf16[8,64,128]{2,1,0:T(8,128)(2,1)S(1)}, u32[]{:S(2)}, u32[]{:S(2)}) async-start(bf16[8,64,128]{2,1,0:T(8,128)(2,1)} %broadcast_in_dim.3), calls=%async_computation | async-start | bytes 262144 | tf_op jit(solution)/shard_map/all_to_all | solution.py:394
  28.3 16.9 %all-to-all-start.1 = ((bf16[8,128,128]{2,1,0:T(8,128)(2,1)}), bf16[8,128,128]{2,1,0:T(8,128)(2,1)S(1)}, u32[]{:S(2)}, u32[]{:S(2)}) async-start(bf16[8,128,128]{2,1,0:T(8,128)(2,1)} %light_pieces.1), calls=%async_computation.1 | async-start | bytes 524288 | tf_op jit(solution)/shard_map/all_to_all | solution.py:383
  35.6 1.4 copy-start
  37.0 0.7 copy-start.3
  37.7 0.7 copy-start.4
  38.4 0.7 copy-start.5
  40.7 16.8 %collective-permute-start = (bf16[512,2048]{1,0:T(8,128)(2,1)S(1)}, bf16[512,2048]{1,0:T(8,128)(2,1)}, u32[]{:S(2)}, u32[]{:S(2)}) collective-permute-start(bf16[512,2048]{1,0:T(8,128)(2,1)S(1)} %dense_blocks.1.mine.refs_2_), channel_id=1, source_target_pairs={{0,1},{1,0},{2,3},{3,2},{4,5},{5,4},{6,7},{7,6},{8,9},{9,8},{10,11... | collective-permute-start | bytes 6291464 | tf_op jit(solution)/shard_map/ppermute | solution.py:409
  46.8 33.6 %all-to-all-start.2 = ((bf16[8,8,64,128]{3,2,1,0:T(8,128)(2,1)}), bf16[8,8,64,128]{3,2,1,0:T(8,128)(2,1)S(1)}, u32[]{:S(2)}, u32[]{:S(2)}) async-start(bf16[8,8,64,128]{3,2,1,0:T(8,128)(2,1)} %heavy_pieces.1), calls=%async_computation.2 | async-start | bytes 2097152 | tf_op jit(solution)/shard_map/all_to_all | solution.py:383
  57.4 41.2 %copy-start.1 = (bf16[256,256]{1,0:T(8,128)(2,1)S(1)}, bf16[256,256]{1,0:T(8,128)(2,1)}, u32[]{:S(2)}) copy-start(bf16[256,256]{1,0:T(8,128)(2,1)} %weight.1) | copy-start | bytes 393220
  57.5 41.2 %copy-start.2 = (bf16[32,256]{1,0:T(8,128)(2,1)S(1)}, bf16[32,256]{1,0:T(8,128)(2,1)}, u32[]{:S(2)}) copy-start(bf16[32,256]{1,0:T(8,128)(2,1)} %cot.1) | copy-start | bytes 49156

commit v4 on v3

--- a/solution.py
+++ b/solution.py
@@ -28,118 +28,86 @@
     return pl.CostEstimate(flops=flops, bytes_accessed=nbytes, transcendentals=0)
 
 
+def wrap(index, size):
+    return jnp.where(index >= size, index - size, index)
+
+
 def dense_kernel(rows, cols, count, tiles, out):
-    section = pl.program_id(0)
-    out[...] = jnp.zeros_like(out)
-    for slot in range(tiles.shape[1]):
-
-        @pl.when(slot < count[section])
-        def _():
-            row = pl.multiple_of(rows[section, slot] * TILE, TILE)
-            col = pl.multiple_of(cols[section, slot] * TILE, TILE)
-            out[pl.ds(row, TILE), pl.ds(col, TILE)] = tiles[0, slot]
+    sections, slots = tiles.shape[:2]
+    span = out.shape[0]
+    for section in range(sections):
+        out[:, section * span : (section + 1) * span] = jnp.zeros((span, span), BF16)
+        for slot in range(slots):
+
+            @pl.when(slot < count[section])
+            def _():
+                row = pl.multiple_of(rows[section, slot] * TILE, TILE)
+                col = pl.multiple_of(section * span + cols[section, slot] * TILE, TILE)
+                out[pl.ds(row, TILE), pl.ds(col, TILE)] = tiles[section, slot]
 
 
 def dense_blocks(tiles, rows, cols, count, rows_blk):
-    sections, slots = tiles.shape[:2]
+    sections = tiles.shape[0]
+    shape = (rows_blk, sections * rows_blk)
     return pl.pallas_call(
         dense_kernel,
-        grid=(sections,),
-        out_shape=shape_of((rows_blk, sections * rows_blk)),
-        in_specs=[
-            SMEM,
-            SMEM,
-            SMEM,
-            pl.BlockSpec((1, slots, TILE, TILE), lambda i: (i, 0, 0, 0)),
-        ],
-        out_specs=pl.BlockSpec((rows_blk, rows_blk), lambda i: (0, i)),
-        compiler_params=params(),
-        cost_estimate=cost(0, tiles.size * 2 + sections * rows_blk * rows_blk * 2),
+        out_shape=shape_of(shape),
+        in_specs=[SMEM, SMEM, SMEM, VMEM],
+        out_specs=VMEM,
+        compiler_params=params(),
+        cost_estimate=cost(0, tiles.size * 2 + math.prod(shape) * 2),
         name="dense_blocks",
     )(rows, cols, count, tiles)
 
 
-def light_kernel(pos, planes, out):
-    ranks, share = planes.shape[:2]
-    first = pos[0] + pos[2]
-    for target in range(ranks):
-        ahead = ((target > pos[1]) & (pos[3] == 1)).astype(jnp.int32)
-        out[target, :share, :] = planes[lax.rem(first + ahead, ranks)]
-        out[target, share:, :] = planes[lax.rem(first + 1, ranks)]
-
-
-def light_pieces(pos, planes):
-    ranks, share, width = planes.shape
-    shape = (ranks, 2 * share, width)
-    return pl.pallas_call(
-        light_kernel,
+def window_kernel(pos, planes, out):
+    ranks = planes.shape[0]
+    plane = [pos[0]]
+    for step in range(ranks):
+        plane.append(wrap(plane[-1] + 1, ranks))
+    for target in range(out.shape[0]):
+        section, rank = target // ranks, target % ranks
+        out[target] = planes[jnp.where(section > pos[1], plane[rank + 1], plane[rank])]
+
+
+def window_pieces(pos, planes, sections):
+    ranks = planes.shape[0]
+    shape = (sections * ranks,) + planes.shape[1:]
+    return pl.pallas_call(
+        window_kernel,
         out_shape=shape_of(shape),
         in_specs=[SMEM, VMEM],
         out_specs=VMEM,
         compiler_params=params(),
         cost_estimate=cost(0, math.prod(shape) * 2),
-        name="light_pieces",
+        name="window_pieces",
     )(pos, planes)
-
-
-def heavy_kernel(pos, parts, out):
-    ranks = parts.shape[0]
-    share = parts.shape[1] // 2
-    for target in range(ranks):
-        ahead = ((target > pos[1]) & (pos[3] == 0)).astype(jnp.int32)
-        start = pl.multiple_of(ahead * share, share)
-        for rank in range(ranks):
-            out[target, rank] = parts[rank, pl.ds(start, share), :]
-
-
-def heavy_pieces(pos, parts):
-    ranks, height, width = parts.shape
-    shape = (ranks, ranks, height // 2, width)
-    return pl.pallas_call(
-        heavy_kernel,
-        out_shape=shape_of(shape),
-        in_specs=[SMEM, VMEM],
-        out_specs=VMEM,
-        compiler_params=params(),
-        cost_estimate=cost(0, math.prod(shape) * 2),
-        name="heavy_pieces",
-    )(pos, parts)
 
 
 def block_order(pos, sections, own, section):
     core = pos[3] if own else 1 - pos[3]
-    return lax.rem(pos[1] + core * (sections // 2) + section, sections)
-
-
-def forward_kernel(pos, mine, other, parts, out, held, sem):
+    return wrap(pos[1] + core * (sections // 2) + section, sections)
+
+
+def forward_kernel(pos, mine, other, blocks, out, held, sem):
     copy = pltpu.make_async_copy(other, held, sem)
     copy.start()
-    ranks = parts.shape[0]
-    flip = pos[3]
-    turned = None
+    sections = blocks.shape[0]
+    total = None
     for is_own, matrix in ((True, mine), (False, held)):
-        slices = []
-        for section in range(ranks // 2):
-            block = block_order(pos, ranks, is_own, section)
-            for rank in range(ranks):
-                outer = jnp.where(flip == 0, block, rank)
-                inner = jnp.where(flip == 0, rank, block)
-                slices.append(parts[outer, inner])
+        side = jnp.concatenate(
+            [blocks[block_order(pos, sections, is_own, i)] for i in range(sections // 2)], axis=0
+        )
         if not is_own:
             copy.wait()
-        product = lax.dot_general(
-            jnp.concatenate(slices, axis=0).T,
-            matrix[...],
-            (((1,), (1,)), ((), ())),
-            preferred_element_type=F32,
-        )
-        turned = product if turned is None else turned + product
-    out[...] = turned.astype(BF16).T
-
-
-def forward_part(pos, mine, other, parts):
+        product = jnp.dot(matrix[...], side, preferred_element_type=F32)
+        total = product if total is None else total + product
+    out[...] = total.astype(BF16)
+
+
+def forward_part(pos, mine, other, blocks):
     rows, columns = mine.shape
-    width = parts.shape[-1]
+    width = blocks.shape[-1]
     return pl.pallas_call(
         forward_kernel,
         out_shape=shape_of((rows, width)),
@@ -147,9 +115,9 @@
         out_specs=VMEM,
         scratch_shapes=[pltpu.VMEM(other.shape, BF16), pltpu.SemaphoreType.DMA],
         compiler_params=params(),
-        cost_estimate=cost(4 * rows * columns * width, 4 * rows * columns + parts.size * 2),
+        cost_estimate=cost(4 * rows * columns * width, 4 * rows * columns + blocks.size * 2),
         name="forward_part",
-    )(pos, mine, other, parts)
+    )(pos, mine, other, blocks)
 
 
 def layer_kernel(pos, parts, cot, weight, act, out, term):
@@ -177,7 +145,7 @@
     for rank in range(ranks):
         for core in (0, 1):
             target = 2 * rank + core
-            row = core * width + lax.rem(pos[0] + rank, ranks) * chunk
+            row = core * width + wrap(pos[0] + rank, ranks) * chunk
             piece = term[pl.ds(pl.multiple_of(row, chunk), chunk), :]
             out[target, :own, :] = dy_value[:, core * width : (core + 1) * width]
             out[target, own : own + chunk, :] = piece[:, :width]
@@ -300,8 +268,8 @@
         far += jnp.where(same, second, first)
         term += parts[source, 2 * share :, :].astype(F32)
     near, far, term = near.astype(BF16), far.astype(BF16), term.astype(BF16)
-    plane = lax.rem(pos[0] + pos[2], ranks)
-    behind = lax.rem(pos[0] + pos[2] + 1, ranks)
+    plane = wrap(pos[0] + pos[2], ranks)
+    behind = wrap(plane + 1, ranks)
     nothing = jnp.zeros_like(near)
     for target in range(ranks):
         value = jnp.where(plane == target, near, jnp.where(behind == target, far, nothing))
@@ -339,7 +307,7 @@
             total += parts[2 * depth + core, :own, :].astype(F32)
         grads[:, core * width : (core + 1) * width] = total.astype(BF16)
         for depth in range(ranks):
-            row = core * width + lax.rem(pos[2] + depth, ranks) * chunk
+            row = core * width + wrap(pos[2] + depth, ranks) * chunk
             for side in (0, 1):
                 first = own + side * chunk
                 value = parts[2 * depth + core, first : first + chunk, :].astype(F32) / scale
@@ -400,20 +368,16 @@
     ranks = lax.axis_size("x")
     share = rows // ranks
     own = share // 2
-    core = lax.axis_index("core")
-    pos = jnp.stack(
-        [lax.axis_index("z"), lax.axis_index("y"), lax.axis_index("x"), core]
-    ).astype(jnp.int32)
+    pos = jnp.stack([lax.axis_index(name) for name in ("z", "y", "x", "core")]).astype(jnp.int32)
 
     mine = dense_blocks(tile_values[0], tile_rows[0], tile_cols[0], tile_count[0], rows)
     other = lax.ppermute(mine, "core", [(0, 1), (1, 0)])
 
-    corner = (lax.axis_index("x") * share, core * width)
+    corner = (lax.axis_index("x") * share, lax.axis_index("core") * width)
     piece = lax.dynamic_slice(features, corner, (share, width))
     planes = exchange(jnp.broadcast_to(piece, (ranks, share, width)), "z")
-    parts = grouped(light_pieces(pos, planes), ranks, ("diagonal", "line"))
-    parts = grouped(heavy_pieces(pos, parts), ranks, ("line", "diagonal"))
-    part = forward_part(pos, mine, other, parts)
+    blocks = exchange(window_pieces(pos, planes, ranks), ("y", "x"))
+    part = forward_part(pos, mine, other, blocks.reshape(ranks, rows, width))
     parts = exchange(part.reshape(2 * ranks, own, width), ("x", "core"))
     activations, pieces = layer_part(pos, parts, cotangent, weight)
     parts = exchange(pieces, ("x", "core"))

time: 184 us -> 172 us (0.935)
  waiting for transfers between devices: 31.6 us -> 25.9 us
  starting transfers between devices: 38.8 us -> 33.4 us
  Pallas kernels: 15.8 us -> 13.5 us
    all_to_all x2 -> x0, waiting for transfers between devices: 23.9 us -> none  [grouped(): lax.all_to_all(pieces, ('z', 'y', 'x', 'core'), split_axis=0, concat_axis...]
    all_to_all x1 -> x2, waiting for transfers between devices: 7.69 us -> 25.9 us  [exchange(): return lax.all_to_all(pieces, axis, split_axis=0, concat_axis=0, tiled=True)]
    all_to_all x2 -> x0, starting transfers between devices: 17.9 us -> none  [grouped(): lax.all_to_all(pieces, ('z', 'y', 'x', 'core'), split_axis=0, concat_axis...]
    all_to_all x1 -> x2, starting transfers between devices: 17.2 us -> 30.4 us  [exchange(): return lax.all_to_all(pieces, axis, split_axis=0, concat_axis=0, tiled=True)]
    all_to_all x3, blocking collectives: 46.5 us -> 50.3 us  [exchange(): return lax.all_to_all(pieces, axis, split_axis=0, concat_axis=0, tiled=True)]
    all_to_all x2, blocking collectives: 45.4 us -> 42.4 us  [grouped(): lax.all_to_all(pieces, ('z', 'y', 'x', 'core'), split_axis=0, concat_axis...]
    pallas_call x3 -> x2, Pallas kernels: 4.5 us -> 2.82 us  [the longest x1 1.61 us: window_pieces(): pl.pallas_call(window_kernel, out_shape=shape_of(shape), in_specs=[SMEM,...]
  transfers between devices with their start and end apart: 4 -> 3, of which waited for: 3 -> 2; matrix products, arithmetic and copies ran while one was open for 0% -> 0% of each run, Pallas kernels for 2% -> 2%
where the time goes in v4:
time: 172 us; the launch traced here: 171 us
  blocking collectives  92.7 us (54%)
  starting transfers between devices  33.4 us (19%)
  waiting for transfers between devices  25.9 us (15%)
  Pallas kernels  13.5 us (8%)
  local copies, waits for them, and re-layouts  4.83 us (3%)
    all_to_all x3, blocking collectives, exchange(): return lax.all_to_all(pieces, axis, split_axis=0, concat_axis=0, tiled=True)  50.3 us
    all_to_all x2, blocking collectives, grouped(): lax.all_to_all(pieces, ('z', 'y', 'x', 'core'), split_axis=0, concat_axis...  42.4 us
    all_to_all x2, starting transfers between devices, exchange(): return lax.all_to_all(pieces, axis, split_axis=0, concat_axis=0, tiled=True)  30.4 us
    all_to_all x2, waiting for transfers between devices, exchange(): return lax.all_to_all(pieces, axis, split_axis=0, concat_axis=0, tiled=True)  25.9 us
  transfers between devices with their start and end apart: 3, of which 2 were waited for; matrix products, arithmetic and copies ran while one was open for 0% of the time, Pallas kernels for 2%

profile of v4, /device:TPU:1, one launch (start us, length us, event | category | flops | bytes accessed | tf_op | source)
XLA Modules:
  0.0 171.1 jit_solution(13461952946994192286)
XLA Ops:
  0.6 0.7 dynamic_slice.3
  1.4 0.7 broadcast_in_dim.3
  2.0 17.2 %all-to-all-start = ((bf16[8,64,128]{2,1,0:T(8,128)(2,1)}), bf16[8,64,128]{2,1,0:T(8,128)(2,1)S(1)}, u32[]{:S(2)}, u32[]{:S(2)}) async-start(bf16[8,64,128]{2,1,0:T(8,128)(2,1)} %broadcast_in_dim.3), calls=%async_computation | async-start | bytes 262144 | tf_op jit(solution)/shard_map/all_to_all | solution.py:362
  19.3 0.0 copy-start
  19.3 1.4 copy-done
  20.7 0.0 copy-start.3
  20.7 0.7 copy-done.3
  21.4 0.0 copy-start.4
  21.4 0.7 copy-done.4
  22.0 0.0 copy-start.5
  22.0 0.7 copy-done.5
  22.7 1.2 dense_blocks.1.mine.refs_2_
  23.9 2.9 %collective-permute-start = (bf16[512,2048]{1,0:T(8,128)(2,1)S(1)}, bf16[512,2048]{1,0:T(8,128)(2,1)}, u32[]{:S(2)}, u32[]{:S(2)}) collective-permute-start(bf16[512,2048]{1,0:T(8,128)(2,1)S(1)} %dense_blocks.1.mine.refs_2_), channel_id=1, source_target_pairs={{0,1},{1,0},{2,3},{3,2},{4,5},{5,4},{6,7},{7,6},{8,9},{9,8},{10,11... | collective-permute-start | bytes 6291464 | tf_op jit(solution)/shard_map/ppermute | solution.py:374
  26.9 0.1 pad_add_fusion.pos.refs_0_
  26.9 0.1 all-to-all-done.planes
  27.0 1.6 window_pieces.1
  28.7 13.2 %all-to-all-start.1 = ((bf16[64,64,128]{2,1,0:T(8,128)(2,1)}), bf16[64,64,128]{2,1,0:T(8,128)(2,1)S(1)}, u32[]{:S(2)}, u32[]{:S(2)}) async-start(bf16[64,64,128]{2,1,0:T(8,128)(2,1)} %window_pieces.1), calls=%async_computation.1 | async-start | bytes 2097152 | tf_op jit(solution)/shard_map/all_to_all | solution.py:362
  41.9 0.0 collective-permute-done.other.refs_3_
  41.9 25.8 %all-to-all-done.1 = bf16[64,64,128]{2,1,0:T(8,128)(2,1)S(1)} async-done(((bf16[64,64,128]{2,1,0:T(8,128)(2,1)}), bf16[64,64,128]{2,1,0:T(8,128)(2,1)S(1)}, u32[]{:S(2)}, u32[]{:S(2)}) %all-to-all-start.1) | async-done | bytes 1048608 | tf_op jit(solution)/shard_map/all_to_all | solution.py:362
  67.7 0.0 copy-start.1
  67.7 0.0 copy-start.2
  67.7 3.4 %forward_part.1 = bf16[512,128]{1,0:T(8,128)(2,1)S(1)} custom-call(s32[4]{0:T(128)S(1)} %pad_add_fusion.pos.refs_0_, bf16[512,2048]{1,0:T(8,128)(2,1)S(1)} %dense_blocks.1.mine.refs_2_, bf16[512,2048]{1,0:T(8,128)(2,1)} %collective-permute-done.other.refs_3_, bf16[8,512,128]{2,1,0:T(8,128)(2,1)S(1)} %bitcast.10), custom_call_target="tpu_custom_call" | custom-call | flops 536870912 | bytes 5242880 | tf_op jit(solution)/shard_map/forward_part/pallas_call | solution.py:111
  71.1 18.6 %all_to_all.35.parts = bf16[16,32,128]{2,1,0:T(8,128)(2,1)S(1)} all-to-all(bf16[16,32,128]{2,1,0:T(8,128)(2,1)S(1)} %bitcast.12), channel_id=1, replica_groups=mesh['z'=8,'y'=8,'x'=8,'core'=2] {'x','core'}, dimensions={0} | all-to-all | bytes 262144 | tf_op jit(solution)/shard_map/all_to_all | solution.py:362
  89.6 0.0 copy-done.1
  89.6 0.0 copy-done.2
  89.6 1.3 layer_part.1
  90.9 14.1 %all_to_all.36.refs_1_ = bf16[16,64,128]{2,1,0:T(8,128)(2,1)S(1)} all-to-all(bf16[16,64,128]{2,1,0:T(8,128)(2,1)S(1)} %get-tuple-element.8), channel_id=1, replica_groups=mesh['z'=8,'y'=8,'x'=8,'core'=2] {'x','core'}, dimensions={0} | all-to-all | bytes 524288 | tf_op jit(solution)/shard_map/all_to_all | solution.py:362
  105.0 3.1 %backward_part.1 = bf16[8,544,128]{2,1,0:T(8,128)(2,1)S(1)} custom-call(s32[4]{0:T(128)S(1)} %pad_add_fusion.pos.refs_0_, bf16[16,64,128]{2,1,0:T(8,128)(2,1)S(1)} %all_to_all.36.refs_1_, bf16[512,2048]{1,0:T(8,128)(2,1)S(1)} %dense_blocks.1.mine.refs_2_, bf16[512,2048]{1,0:T(8,128)(2,1)} %collective-permute-done.other.refs_3_), custom_call_target="tpu_custom_call" | custom-call | flops 536870912 | bytes 5308416 | tf_op jit(solution)/shard_map/backward_part/pallas_call | solution.py:207
  108.2 29.4 %all_to_all.37.refs_1_ = bf16[8,544,128]{2,1,0:T(8,128)(2,1)S(1)} all-to-all(bf16[8,544,128]{2,1,0:T(8,128)(2,1)S(1)} %backward_part.1), channel_id=1, replica_groups={{0,16,32,48,64,80,96,112},{2,18,34,50,66,82,98,114},{4,20,36,52,68,84,1..., dimensions={0} | all-to-all | bytes 2228224 | tf_op jit(solution)/shard_map/all_to_all | solution.py:351
  137.5 0.9 merge_part.1
  138.5 13.0 %all_to_all.38.refs_1_ = bf16[8,160,128]{2,1,0:T(8,128)(2,1)S(1)} all-to-all(bf16[8,160,128]{2,1,0:T(8,128)(2,1)S(1)} %merge_part.1), channel_id=1, replica_groups={{0,898,772,646,520,394,268,142},{16,914,788,662,536,410,284,158},{32,93..., dimensions={0} | all-to-all | bytes 655360 | tf_op jit(solution)/shard_map/all_to_all | solution.py:351
  151.5 0.6 place_part.1
  152.1 17.6 %all_to_all.39.refs_1_ = bf16[16,64,128]{2,1,0:T(8,128)(2,1)S(1)} all-to-all(bf16[16,64,128]{2,1,0:T(8,128)(2,1)S(1)} %place_part.1), channel_id=1, replica_groups=mesh['z'=8,'y'=8,'x'=8,'core'=2] {'z','core'}, dimensions={0} | all-to-all | bytes 524288 | tf_op jit(solution)/shard_map/all_to_all | solution.py:362
  169.8 1.3 finish_part.1
Async XLA Ops:
  2.0 25.0 %all-to-all-start = ((bf16[8,64,128]{2,1,0:T(8,128)(2,1)}), bf16[8,64,128]{2,1,0:T(8,128)(2,1)S(1)}, u32[]{:S(2)}, u32[]{:S(2)}) async-start(bf16[8,64,128]{2,1,0:T(8,128)(2,1)} %broadcast_in_dim.3), calls=%async_computation | async-start | bytes 262144 | tf_op jit(solution)/shard_map/all_to_all | solution.py:362
  19.3 1.4 copy-start
  20.7 0.7 copy-start.3
  21.4 0.7 copy-start.4
  22.0 0.7 copy-start.5
  23.9 18.0 %collective-permute-start = (bf16[512,2048]{1,0:T(8,128)(2,1)S(1)}, bf16[512,2048]{1,0:T(8,128)(2,1)}, u32[]{:S(2)}, u32[]{:S(2)}) collective-permute-start(bf16[512,2048]{1,0:T(8,128)(2,1)S(1)} %dense_blocks.1.mine.refs_2_), channel_id=1, source_target_pairs={{0,1},{1,0},{2,3},{3,2},{4,5},{5,4},{6,7},{7,6},{8,9},{9,8},{10,11... | collective-permute-start | bytes 6291464 | tf_op jit(solution)/shard_map/ppermute | solution.py:374
  28.7 39.0 %all-to-all-start.1 = ((bf16[64,64,128]{2,1,0:T(8,128)(2,1)}), bf16[64,64,128]{2,1,0:T(8,128)(2,1)S(1)}, u32[]{:S(2)}, u32[]{:S(2)}) async-start(bf16[64,64,128]{2,1,0:T(8,128)(2,1)} %window_pieces.1), calls=%async_computation.1 | async-start | bytes 2097152 | tf_op jit(solution)/shard_map/all_to_all | solution.py:362
  67.7 22.0 %copy-start.1 = (bf16[256,256]{1,0:T(8,128)(2,1)S(1)}, bf16[256,256]{1,0:T(8,128)(2,1)}, u32[]{:S(2)}) copy-start(bf16[256,256]{1,0:T(8,128)(2,1)} %weight.1) | copy-start | bytes 393220
  67.7 22.0 %copy-start.2 = (bf16[32,256]{1,0:T(8,128)(2,1)S(1)}, bf16[32,256]{1,0:T(8,128)(2,1)}, u32[]{:S(2)}) copy-start(bf16[32,256]{1,0:T(8,128)(2,1)} %cot.1) | copy-start | bytes 49156

commit v5 on v4

--- a/solution.py
+++ b/solution.py
@@ -32,42 +32,43 @@
     return jnp.where(index >= size, index - size, index)
 
 
-def dense_kernel(rows, cols, count, tiles, out):
+def dense_kernel(index, tiles, out):
     sections, slots = tiles.shape[:2]
     span = out.shape[0]
     for section in range(sections):
         out[:, section * span : (section + 1) * span] = jnp.zeros((span, span), BF16)
         for slot in range(slots):
 
-            @pl.when(slot < count[section])
+            @pl.when(slot < index[section, 2 * slots])
             def _():
-                row = pl.multiple_of(rows[section, slot] * TILE, TILE)
-                col = pl.multiple_of(section * span + cols[section, slot] * TILE, TILE)
+                row = pl.multiple_of(index[section, slot] * TILE, TILE)
+                col = pl.multiple_of(section * span + index[section, slots + slot] * TILE, TILE)
                 out[pl.ds(row, TILE), pl.ds(col, TILE)] = tiles[section, slot]
 
 
 def dense_blocks(tiles, rows, cols, count, rows_blk):
     sections = tiles.shape[0]
     shape = (rows_blk, sections * rows_blk)
+    index = jnp.concatenate([rows, cols, count[:, None]], axis=1)
     return pl.pallas_call(
         dense_kernel,
         out_shape=shape_of(shape),
-        in_specs=[SMEM, SMEM, SMEM, VMEM],
+        in_specs=[SMEM, VMEM],
         out_specs=VMEM,
         compiler_params=params(),
         cost_estimate=cost(0, tiles.size * 2 + math.prod(shape) * 2),
         name="dense_blocks",
-    )(rows, cols, count, tiles)
+    )(index, tiles)
 
 
 def window_kernel(pos, planes, out):
     ranks = planes.shape[0]
-    plane = [pos[0]]
+    place = [pos[2]]
     for step in range(ranks):
-        plane.append(wrap(plane[-1] + 1, ranks))
+        place.append(wrap(place[-1] + 1, ranks))
     for target in range(out.shape[0]):
-        section, rank = target // ranks, target % ranks
-        out[target] = planes[jnp.where(section > pos[1], plane[rank + 1], plane[rank])]
+        section, step = target // ranks, target % ranks
+        out[target] = planes[jnp.where(section > pos[1], place[step + 1], place[step])]
 
 
 def window_pieces(pos, planes, sections):
@@ -178,28 +179,28 @@
     for source in range(1, replicas):
         piece += parts[source, own:, :].astype(F32)
     piece = piece.astype(BF16)
+    height = out.shape[0] // ranks
     for target in range(ranks):
-        out[target, rows:, :] = piece
+        out[target * height + rows : (target + 1) * height, :] = piece
     dy_turned = parts[:, :own, :].reshape(rows, width).T
-    flip = pos[3]
+    by_block = jnp.where(pos[3] == 0, height, share)
+    by_rank = jnp.where(pos[3] == 0, share, height)
     for is_own, matrix in ((True, mine), (False, held)):
         if not is_own:
             copy.wait()
         for section in range(ranks // 2):
             side = matrix[:, section * rows : (section + 1) * rows]
             grads = jnp.dot(dy_turned, side, preferred_element_type=F32).astype(BF16).T
-            block = block_order(pos, ranks, is_own, section)
+            first = block_order(pos, ranks, is_own, section) * by_block
             for rank in range(ranks):
-                outer = jnp.where(flip == 0, block, rank)
-                inner = jnp.where(flip == 0, rank, block)
-                start = pl.multiple_of(inner * share, share)
-                out[outer, pl.ds(start, share), :] = grads[rank * share : (rank + 1) * share, :]
+                start = pl.multiple_of(first + rank * by_rank, 16)
+                out[pl.ds(start, share), :] = grads[rank * share : (rank + 1) * share, :]
 
 
 def backward_part(pos, parts, mine, other, own):
     replicas, height, width = parts.shape
     rows, columns = mine.shape
-    out = (replicas // 2, rows + height - own, width)
+    out = (replicas // 2 * (rows + height - own), width)
 
     def kernel(*refs):
         backward_kernel(own, *refs)
@@ -335,25 +336,46 @@
     return ((depth % ranks * ranks + section) * ranks + rank) * 2 + core
 
 
-def groups(ranks, kinds):
-    found = []
-    for core, kind in enumerate(kinds):
-        for a in range(ranks):
-            for b in range(ranks):
-                if kind == "line":
-                    found.append([device_at(ranks, a, k, b, core) for k in range(ranks)])
-                else:
-                    found.append([device_at(ranks, a - k, b, k, core) for k in range(ranks)])
-    return found
-
-
-def grouped(pieces, ranks, kinds):
+def section_groups(ranks):
+    every = [(a, b) for a in range(ranks) for b in range(ranks)]
+    steps = range(ranks)
+    line = [[device_at(ranks, a, k, b, 0) for k in steps] for a, b in every]
+    slant = [[device_at(ranks, a - k, b, k, 1) for k in steps] for a, b in every]
+    return line + slant
+
+
+def share_groups(ranks):
+    return [[device ^ 1 for device in group] for group in section_groups(ranks)]
+
+
+def plane_groups(ranks):
+    return [
+        [device_at(ranks, i - rank, section, rank, core) for i in range(ranks)]
+        for section in range(ranks)
+        for rank in range(ranks)
+        for core in (0, 1)
+    ]
+
+
+def window_groups(ranks):
+    return [
+        [
+            device_at(ranks, depth, section, (i - depth) % ranks, core)
+            for section in range(ranks)
+            for i in range(ranks)
+        ]
+        for depth in range(ranks)
+        for core in (0, 1)
+    ]
+
+
+def grouped(pieces, lists):
     return lax.all_to_all(
         pieces,
         ("z", "y", "x", "core"),
         split_axis=0,
         concat_axis=0,
-        axis_index_groups=groups(ranks, kinds),
+        axis_index_groups=lists,
         tiled=True,
     )
 
@@ -373,17 +395,17 @@
     mine = dense_blocks(tile_values[0], tile_rows[0], tile_cols[0], tile_count[0], rows)
     other = lax.ppermute(mine, "core", [(0, 1), (1, 0)])
 
-    corner = (lax.axis_index("x") * share, lax.axis_index("core") * width)
-    piece = lax.dynamic_slice(features, corner, (share, width))
-    planes = exchange(jnp.broadcast_to(piece, (ranks, share, width)), "z")
-    blocks = exchange(window_pieces(pos, planes, ranks), ("y", "x"))
+    half = lax.dynamic_slice_in_dim(features, lax.axis_index("core") * width, width, axis=1)
+    planes = grouped(half.reshape(ranks, share, width), plane_groups(ranks))
+    planes, other = lax.optimization_barrier((planes, other))
+    blocks = grouped(window_pieces(pos, planes, ranks), window_groups(ranks))
     part = forward_part(pos, mine, other, blocks.reshape(ranks, rows, width))
     parts = exchange(part.reshape(2 * ranks, own, width), ("x", "core"))
     activations, pieces = layer_part(pos, parts, cotangent, weight)
     parts = exchange(pieces, ("x", "core"))
     pieces = backward_part(pos, parts, mine, other, own)
-    parts = grouped(pieces, ranks, ("line", "diagonal"))
-    parts = grouped(merge_part(pos, parts, rows), ranks, ("diagonal", "line"))
+    parts = grouped(pieces, section_groups(ranks)).reshape(ranks, -1, width)
+    parts = grouped(merge_part(pos, parts, rows), share_groups(ranks))
     parts = exchange(place_part(pos, parts, share), ("z", "core"))
     weight_grad, feature_grad = finish_part(pos, parts, own, rows * ranks * ranks)
     return (activations, weight_grad, feature_grad)

time: 172 us -> 175 us (1.017)
  blocking collectives: 92.7 us -> 129 us
  waiting for transfers between devices: 25.9 us -> 8.44 us
  starting transfers between devices: 33.4 us -> 19.8 us
  local copies, waits for them, and re-layouts: 4.83 us -> 2.88 us
    all_to_all x2 -> x3, blocking collectives: 42.4 us -> 78.7 us  [grouped(): lax.all_to_all(pieces, ('z', 'y', 'x', 'core'), split_axis=0, concat_axis...]
    all_to_all x2 -> x1, starting transfers between devices: 30.4 us -> 3.66 us  [grouped(): lax.all_to_all(pieces, ('z', 'y', 'x', 'core'), split_axis=0, concat_axis...]
    all_to_all x2 -> x1, waiting for transfers between devices: 25.9 us -> 8.43 us  [grouped(): lax.all_to_all(pieces, ('z', 'y', 'x', 'core'), split_axis=0, concat_axis...]
    ppermute x1, starting transfers between devices: 2.93 us -> 16.1 us  [per_device(): other = lax.ppermute(mine, 'core', [(0, 1), (1, 0)])]
    unnamed x12 -> x8, local copies, waits for them, and re-layouts: 3.43 us -> 1.43 us
  transfers between devices with their start and end apart: 3 -> 2, of which waited for: 2 -> 1; matrix products, arithmetic and copies ran while one was open for 0% -> 0% of each run, Pallas kernels for 2% -> 0%
where the time goes in v5:
time: 175 us; the launch traced here: 174 us
  blocking collectives  129 us (74%)
  starting transfers between devices  19.8 us (11%)
  Pallas kernels  12.6 us (7%)
  waiting for transfers between devices  8.44 us (5%)
  local copies, waits for them, and re-layouts  2.88 us (2%)
    all_to_all x3, blocking collectives, grouped(): lax.all_to_all(pieces, ('z', 'y', 'x', 'core'), split_axis=0, concat_axis...  78.7 us
    all_to_all x3, blocking collectives, exchange(): return lax.all_to_all(pieces, axis, split_axis=0, concat_axis=0, tiled=True)  50.3 us
    ppermute x1, starting transfers between devices, per_device(): other = lax.ppermute(mine, 'core', [(0, 1), (1, 0)])  16.1 us
    all_to_all x1, waiting for transfers between devices, grouped(): lax.all_to_all(pieces, ('z', 'y', 'x', 'core'), split_axis=0, concat_axis...  8.43 us
    all_to_all x1, starting transfers between devices, grouped(): lax.all_to_all(pieces, ('z', 'y', 'x', 'core'), split_axis=0, concat_axis...  3.66 us
  transfers between devices with their start and end apart: 2, of which 1 were waited for; matrix products, arithmetic and copies ran while one was open for 0% of the time, Pallas kernels for 0%

profile of v5, /device:TPU:1, one launch (start us, length us, event | category | flops | bytes accessed | tf_op | source)
XLA Modules:
  0.0 174.2 jit_solution(14061684506124959592)
XLA Ops:
  0.6 0.0 copy-start
  0.6 0.8 copy.10
  1.4 0.8 pad_add_fusion.index
  2.2 0.0 copy-start.1
  2.2 1.4 copy-done.1
  3.6 1.3 dense_blocks.1.mine.refs_2_
  4.9 16.1 %collective-permute-start = (bf16[512,2048]{1,0:T(8,128)(2,1)S(1)}, bf16[512,2048]{1,0:T(8,128)(2,1)}, u32[]{:S(2)}, u32[]{:S(2)}) collective-permute-start(bf16[512,2048]{1,0:T(8,128)(2,1)S(1)} %dense_blocks.1.mine.refs_2_), channel_id=1, source_target_pairs={{0,1},{1,0},{2,3},{3,2},{4,5},{5,4},{6,7},{7,6},{8,9},{9,8},{10,11... | collective-permute-start | bytes 6291464 | tf_op jit(solution)/shard_map/ppermute | solution.py:396
  21.0 0.0 copy-done
  21.0 0.7 constant_dynamic-slice_fusion
  21.7 3.7 %all-to-all-start = ((bf16[8,64,128]{2,1,0:T(8,128)(2,1)}), bf16[8,64,128]{2,1,0:T(8,128)(2,1)S(1)}, u32[]{:S(2)}, u32[]{:S(2)}) async-start(bf16[8,64,128]{2,1,0:T(8,128)(2,1)} %bitcast.8), calls=%async_computation | async-start | bytes 262144 | tf_op jit(solution)/shard_map/all_to_all | solution.py:373
  25.4 0.1 pad_add_fusion.1.pos.refs_0_
  25.4 8.4 %all-to-all-done.planes = bf16[8,64,128]{2,1,0:T(8,128)(2,1)S(1)} async-done(((bf16[8,64,128]{2,1,0:T(8,128)(2,1)}), bf16[8,64,128]{2,1,0:T(8,128)(2,1)S(1)}, u32[]{:S(2)}, u32[]{:S(2)}) %all-to-all-start) | async-done | bytes 131104 | tf_op jit(solution)/shard_map/all_to_all | solution.py:373
  33.9 0.0 collective-permute-done.other.refs_3_
  33.9 0.6 window_pieces.1
  34.5 39.3 %all_to_all.39 = bf16[64,64,128]{2,1,0:T(8,128)(2,1)S(1)} all-to-all(bf16[64,64,128]{2,1,0:T(8,128)(2,1)S(1)} %window_pieces.1), channel_id=1, replica_groups={{0,2,4,6,8,10,12,14,16,18,20,22,24,26,28,30,32,34,36,38,40,42,44,46,48,..., dimensions={0} | all-to-all | bytes 2097152 | tf_op jit(solution)/shard_map/all_to_all | solution.py:373
  73.9 0.0 copy-start.2
  73.9 0.0 copy-start.3
  73.9 3.4 %forward_part.1 = bf16[512,128]{1,0:T(8,128)(2,1)S(1)} custom-call(s32[4]{0:T(128)S(1)} %pad_add_fusion.1.pos.refs_0_, bf16[512,2048]{1,0:T(8,128)(2,1)S(1)} %dense_blocks.1.mine.refs_2_, bf16[512,2048]{1,0:T(8,128)(2,1)} %collective-permute-done.other.refs_3_, bf16[8,512,128]{2,1,0:T(8,128)(2,1)S(1)} %bitcast.13), custom_call_target="tpu_custom_call" | custom-call | flops 536870912 | bytes 5242880 | tf_op jit(solution)/shard_map/forward_part/pallas_call | solution.py:112
  77.3 17.4 %all_to_all.40.parts = bf16[16,32,128]{2,1,0:T(8,128)(2,1)S(1)} all-to-all(bf16[16,32,128]{2,1,0:T(8,128)(2,1)S(1)} %bitcast.15), channel_id=1, replica_groups=mesh['z'=8,'y'=8,'x'=8,'core'=2] {'x','core'}, dimensions={0} | all-to-all | bytes 262144 | tf_op jit(solution)/shard_map/all_to_all | solution.py:384
  94.7 0.0 copy-done.2
  94.7 0.0 copy-done.3
  94.7 1.3 layer_part.1
  96.0 14.1 %all_to_all.41.refs_1_ = bf16[16,64,128]{2,1,0:T(8,128)(2,1)S(1)} all-to-all(bf16[16,64,128]{2,1,0:T(8,128)(2,1)S(1)} %get-tuple-element.12), channel_id=1, replica_groups=mesh['z'=8,'y'=8,'x'=8,'core'=2] {'x','core'}, dimensions={0} | all-to-all | bytes 524288 | tf_op jit(solution)/shard_map/all_to_all | solution.py:384
  110.1 3.1 %backward_part.1 = bf16[4352,128]{1,0:T(8,128)(2,1)S(1)} custom-call(s32[4]{0:T(128)S(1)} %pad_add_fusion.1.pos.refs_0_, bf16[16,64,128]{2,1,0:T(8,128)(2,1)S(1)} %all_to_all.41.refs_1_, bf16[512,2048]{1,0:T(8,128)(2,1)S(1)} %dense_blocks.1.mine.refs_2_, bf16[512,2048]{1,0:T(8,128)(2,1)} %collective-permute-done.other.refs_3_), custom_call_target="tpu_custom_call" | custom-call | flops 536870912 | bytes 5308416 | tf_op jit(solution)/shard_map/backward_part/pallas_call | solution.py:208
  113.3 25.8 %all_to_all.42.refs_1_ = bf16[8,544,128]{2,1,0:T(8,128)(2,1)S(1)} all-to-all(bf16[8,544,128]{2,1,0:T(8,128)(2,1)S(1)} %bitcast.12), channel_id=1, replica_groups={{0,16,32,48,64,80,96,112},{2,18,34,50,66,82,98,114},{4,20,36,52,68,84,1..., dimensions={0} | all-to-all | bytes 2228224 | tf_op jit(solution)/shard_map/all_to_all | solution.py:373
  139.0 0.9 merge_part.1
  140.0 13.6 %all_to_all.43.refs_1_ = bf16[8,160,128]{2,1,0:T(8,128)(2,1)S(1)} all-to-all(bf16[8,160,128]{2,1,0:T(8,128)(2,1)S(1)} %merge_part.1), channel_id=1, replica_groups={{1,17,33,49,65,81,97,113},{3,19,35,51,67,83,99,115},{5,21,37,53,69,85,1..., dimensions={0} | all-to-all | bytes 655360 | tf_op jit(solution)/shard_map/all_to_all | solution.py:373
  153.5 0.6 place_part.1
  154.2 18.8 %all_to_all.44.refs_1_ = bf16[16,64,128]{2,1,0:T(8,128)(2,1)S(1)} all-to-all(bf16[16,64,128]{2,1,0:T(8,128)(2,1)S(1)} %place_part.1), channel_id=1, replica_groups=mesh['z'=8,'y'=8,'x'=8,'core'=2] {'z','core'}, dimensions={0} | all-to-all | bytes 524288 | tf_op jit(solution)/shard_map/all_to_all | solution.py:384
  172.9 1.3 finish_part.1
Async XLA Ops:
  0.6 20.4 %copy-start = (bf16[512,256]{1,0:T(8,128)(2,1)S(1)}, bf16[512,256]{1,0:T(8,128)(2,1)}, u32[]{:S(2)}) copy-start(bf16[512,256]{1,0:T(8,128)(2,1)} %param.7) | copy-start | bytes 786436
  2.2 1.4 copy-start.1
  4.9 29.0 %collective-permute-start = (bf16[512,2048]{1,0:T(8,128)(2,1)S(1)}, bf16[512,2048]{1,0:T(8,128)(2,1)}, u32[]{:S(2)}, u32[]{:S(2)}) collective-permute-start(bf16[512,2048]{1,0:T(8,128)(2,1)S(1)} %dense_blocks.1.mine.refs_2_), channel_id=1, source_target_pairs={{0,1},{1,0},{2,3},{3,2},{4,5},{5,4},{6,7},{7,6},{8,9},{9,8},{10,11... | collective-permute-start | bytes 6291464 | tf_op jit(solution)/shard_map/ppermute | solution.py:396
  21.7 12.2 %all-to-all-start = ((bf16[8,64,128]{2,1,0:T(8,128)(2,1)}), bf16[8,64,128]{2,1,0:T(8,128)(2,1)S(1)}, u32[]{:S(2)}, u32[]{:S(2)}) async-start(bf16[8,64,128]{2,1,0:T(8,128)(2,1)} %bitcast.8), calls=%async_computation | async-start | bytes 262144 | tf_op jit(solution)/shard_map/all_to_all | solution.py:373
  73.9 20.8 %copy-start.2 = (bf16[256,256]{1,0:T(8,128)(2,1)S(1)}, bf16[256,256]{1,0:T(8,128)(2,1)}, u32[]{:S(2)}) copy-start(bf16[256,256]{1,0:T(8,128)(2,1)} %weight.1) | copy-start | bytes 393220
  73.9 20.8 %copy-start.3 = (bf16[32,256]{1,0:T(8,128)(2,1)S(1)}, bf16[32,256]{1,0:T(8,128)(2,1)}, u32[]{:S(2)}) copy-start(bf16[32,256]{1,0:T(8,128)(2,1)} %cot.1) | copy-start | bytes 49156

commit v6 on v5

--- a/solution.py
+++ b/solution.py
@@ -13,7 +13,6 @@
 F32 = jnp.float32
 VMEM = pl.BlockSpec(memory_space=pltpu.VMEM)
 SMEM = pl.BlockSpec(memory_space=pltpu.SMEM)
-ANY = pl.BlockSpec(memory_space=pl.ANY)
 
 
 def params(mib=40):
@@ -32,33 +31,32 @@
     return jnp.where(index >= size, index - size, index)
 
 
-def dense_kernel(index, tiles, out):
+def dense_kernel(rows, cols, count, tiles, out):
     sections, slots = tiles.shape[:2]
     span = out.shape[0]
     for section in range(sections):
         out[:, section * span : (section + 1) * span] = jnp.zeros((span, span), BF16)
         for slot in range(slots):
 
-            @pl.when(slot < index[section, 2 * slots])
+            @pl.when(slot < count[section])
             def _():
-                row = pl.multiple_of(index[section, slot] * TILE, TILE)
-                col = pl.multiple_of(section * span + index[section, slots + slot] * TILE, TILE)
+                row = pl.multiple_of(rows[section, slot] * TILE, TILE)
+                col = pl.multiple_of(section * span + cols[section, slot] * TILE, TILE)
                 out[pl.ds(row, TILE), pl.ds(col, TILE)] = tiles[section, slot]
 
 
 def dense_blocks(tiles, rows, cols, count, rows_blk):
     sections = tiles.shape[0]
     shape = (rows_blk, sections * rows_blk)
-    index = jnp.concatenate([rows, cols, count[:, None]], axis=1)
     return pl.pallas_call(
         dense_kernel,
         out_shape=shape_of(shape),
-        in_specs=[SMEM, VMEM],
+        in_specs=[SMEM, SMEM, SMEM, VMEM],
         out_specs=VMEM,
         compiler_params=params(),
         cost_estimate=cost(0, tiles.size * 2 + math.prod(shape) * 2),
         name="dense_blocks",
-    )(index, tiles)
+    )(rows, cols, count, tiles)
 
 
 def window_kernel(pos, planes, out):
@@ -90,17 +88,13 @@
     return wrap(pos[1] + core * (sections // 2) + section, sections)
 
 
-def forward_kernel(pos, mine, other, blocks, out, held, sem):
-    copy = pltpu.make_async_copy(other, held, sem)
-    copy.start()
+def forward_kernel(pos, mine, other, blocks, out):
     sections = blocks.shape[0]
     total = None
-    for is_own, matrix in ((True, mine), (False, held)):
+    for is_own, matrix in ((True, mine), (False, other)):
         side = jnp.concatenate(
             [blocks[block_order(pos, sections, is_own, i)] for i in range(sections // 2)], axis=0
         )
-        if not is_own:
-            copy.wait()
         product = jnp.dot(matrix[...], side, preferred_element_type=F32)
         total = product if total is None else total + product
     out[...] = total.astype(BF16)
@@ -112,16 +106,15 @@
     return pl.pallas_call(
         forward_kernel,
         out_shape=shape_of((rows, width)),
-        in_specs=[SMEM, VMEM, ANY, VMEM],
-        out_specs=VMEM,
-        scratch_shapes=[pltpu.VMEM(other.shape, BF16), pltpu.SemaphoreType.DMA],
+        in_specs=[SMEM, VMEM, VMEM, VMEM],
+        out_specs=VMEM,
         compiler_params=params(),
         cost_estimate=cost(4 * rows * columns * width, 4 * rows * columns + blocks.size * 2),
         name="forward_part",
     )(pos, mine, other, blocks)
 
 
-def layer_kernel(pos, parts, cot, weight, act, out, term):
+def layer_kernel(parts, cot, weight, act, out):
     replicas, own, width = parts.shape
     ranks = replicas // 2
     sides = []
@@ -139,38 +132,34 @@
     dy_value = lax.dot_general(
         dz_value, weight[...], (((1,), (1,)), ((), ())), preferred_element_type=F32
     ).astype(BF16)
-    term[...] = lax.dot_general(
+    term = lax.dot_general(
         agg, dz_value, (((0,), (0,)), ((), ())), preferred_element_type=F32
     ).astype(BF16)
     chunk = width // ranks
     for rank in range(ranks):
         for core in (0, 1):
             target = 2 * rank + core
-            row = core * width + wrap(pos[0] + rank, ranks) * chunk
-            piece = term[pl.ds(pl.multiple_of(row, chunk), chunk), :]
+            row = core * width + rank * chunk
             out[target, :own, :] = dy_value[:, core * width : (core + 1) * width]
-            out[target, own : own + chunk, :] = piece[:, :width]
-            out[target, own + chunk :, :] = piece[:, width:]
-
-
-def layer_part(pos, parts, cot, weight):
+            out[target, own : own + chunk, :] = term[row : row + chunk, :width]
+            out[target, own + chunk :, :] = term[row : row + chunk, width:]
+
+
+def layer_part(parts, cot, weight):
     replicas, own, width = parts.shape
     out = (replicas, own + 4 * width // replicas, width)
     return pl.pallas_call(
         layer_kernel,
         out_shape=(shape_of(cot.shape), shape_of(out)),
-        in_specs=[SMEM, VMEM, VMEM, VMEM],
+        in_specs=[VMEM] * 3,
         out_specs=(VMEM, VMEM),
-        scratch_shapes=[pltpu.VMEM(weight.shape, BF16)],
         compiler_params=params(),
         cost_estimate=cost(6 * own * 4 * width * width, math.prod(out) * 4),
         name="layer_part",
-    )(pos, parts, cot, weight)
-
-
-def backward_kernel(own, pos, parts, mine, other, out, held, sem):
-    copy = pltpu.make_async_copy(other, held, sem)
-    copy.start()
+    )(parts, cot, weight)
+
+
+def backward_kernel(own, pos, parts, mine, other, out):
     replicas, _, width = parts.shape
     ranks = replicas // 2
     rows = replicas * own
@@ -182,12 +171,14 @@
     height = out.shape[0] // ranks
     for target in range(ranks):
         out[target * height + rows : (target + 1) * height, :] = piece
-    dy_turned = parts[:, :own, :].reshape(rows, width).T
+    chunks = []
+    for rank in range(ranks):
+        place = 2 * wrap(pos[0] + rank, ranks)
+        chunks += [parts[place, :own, :], parts[place + 1, :own, :]]
+    dy_turned = jnp.concatenate(chunks, axis=0).T
     by_block = jnp.where(pos[3] == 0, height, share)
     by_rank = jnp.where(pos[3] == 0, share, height)
-    for is_own, matrix in ((True, mine), (False, held)):
-        if not is_own:
-            copy.wait()
+    for is_own, matrix in ((True, mine), (False, other)):
         for section in range(ranks // 2):
             side = matrix[:, section * rows : (section + 1) * rows]
             grads = jnp.dot(dy_turned, side, preferred_element_type=F32).astype(BF16).T
@@ -208,9 +199,8 @@
     return pl.pallas_call(
         kernel,
         out_shape=shape_of(out),
-        in_specs=[SMEM, VMEM, VMEM, ANY],
-        out_specs=VMEM,
-        scratch_shapes=[pltpu.VMEM(other.shape, BF16), pltpu.SemaphoreType.DMA],
+        in_specs=[SMEM, VMEM, VMEM, VMEM],
+        out_specs=VMEM,
         compiler_params=params(),
         cost_estimate=cost(4 * rows * columns * width, 4 * rows * columns + math.prod(out) * 2),
         name="backward_part",
@@ -369,6 +359,18 @@
     ]
 
 
+def replica_groups(ranks):
+    return [
+        [
+            device_at(ranks, depth, section, (i - depth) % ranks, core)
+            for i in range(ranks)
+            for core in (0, 1)
+        ]
+        for depth in range(ranks)
+        for section in range(ranks)
+    ]
+
+
 def grouped(pieces, lists):
     return lax.all_to_all(
         pieces,
@@ -392,17 +394,19 @@
     own = share // 2
     pos = jnp.stack([lax.axis_index(name) for name in ("z", "y", "x", "core")]).astype(jnp.int32)
 
+    half = lax.dynamic_slice_in_dim(features, lax.axis_index("core") * width, width, axis=1)
+    half, tile_rows, tile_cols, tile_count = lax.optimization_barrier(
+        (half, tile_rows, tile_cols, tile_count)
+    )
+    planes = grouped(half.reshape(ranks, share, width), plane_groups(ranks))
     mine = dense_blocks(tile_values[0], tile_rows[0], tile_cols[0], tile_count[0], rows)
+    pieces, mine = lax.optimization_barrier((window_pieces(pos, planes, ranks), mine))
     other = lax.ppermute(mine, "core", [(0, 1), (1, 0)])
-
-    half = lax.dynamic_slice_in_dim(features, lax.axis_index("core") * width, width, axis=1)
-    planes = grouped(half.reshape(ranks, share, width), plane_groups(ranks))
-    planes, other = lax.optimization_barrier((planes, other))
-    blocks = grouped(window_pieces(pos, planes, ranks), window_groups(ranks))
+    blocks = grouped(pieces, window_groups(ranks))
     part = forward_part(pos, mine, other, blocks.reshape(ranks, rows, width))
     parts = exchange(part.reshape(2 * ranks, own, width), ("x", "core"))
-    activations, pieces = layer_part(pos, parts, cotangent, weight)
-    parts = exchange(pieces, ("x", "core"))
+    activations, pieces = layer_part(parts, cotangent, weight)
+    parts = grouped(pieces, replica_groups(ranks))
     pieces = backward_part(pos, parts, mine, other, own)
     parts = grouped(pieces, section_groups(ranks)).reshape(ranks, -1, width)
     parts = grouped(merge_part(pos, parts, rows), share_groups(ranks))

time: 175 us -> 169 us (0.966)
  waiting for transfers between devices: 8.44 us -> 3.04 us
  Pallas kernels: 12.6 us -> 8.66 us
  local copies, waits for them, and re-layouts: 2.88 us -> 5.04 us
    all_to_all x3 -> x4, blocking collectives: 78.7 us -> 97.3 us  [grouped(): lax.all_to_all(pieces, ('z', 'y', 'x', 'core'), split_axis=0, concat_axis...]
    all_to_all x3 -> x2, blocking collectives: 50.3 us -> 32.3 us  [exchange(): return lax.all_to_all(pieces, axis, split_axis=0, concat_axis=0, tiled=True)]
    all_to_all x1, starting transfers between devices: 3.66 us -> 17.2 us  [grouped(): lax.all_to_all(pieces, ('z', 'y', 'x', 'core'), split_axis=0, concat_axis...]
    ppermute x1, starting transfers between devices: 16.1 us -> 4.19 us  [per_device(): other = lax.ppermute(mine, 'core', [(0, 1), (1, 0)])]
    all_to_all x1, waiting for transfers between devices: 8.43 us -> 3.03 us  [grouped(): lax.all_to_all(pieces, ('z', 'y', 'x', 'core'), split_axis=0, concat_axis...]
    unnamed x8 -> x14, local copies, waits for them, and re-layouts: 1.43 us -> 4.37 us
  transfers between devices with their start and end apart: 2 -> 2, of which waited for: 1 -> 1; matrix products, arithmetic and copies ran while one was open for 0% -> 0% of each run, Pallas kernels for 0% -> 1%
where the time goes in v6:
time: 169 us
  blocking collectives  130 us (77%)
  starting transfers between devices  21.4 us (13%)
  Pallas kernels  8.66 us (5%)
  local copies, waits for them, and re-layouts  5.04 us (3%)
  waiting for transfers between devices  3.04 us (2%)
    all_to_all x4, blocking collectives, grouped(): lax.all_to_all(pieces, ('z', 'y', 'x', 'core'), split_axis=0, concat_axis...  97.3 us
    all_to_all x2, blocking collectives, exchange(): return lax.all_to_all(pieces, axis, split_axis=0, concat_axis=0, tiled=True)  32.3 us
    all_to_all x1, starting transfers between devices, grouped(): lax.all_to_all(pieces, ('z', 'y', 'x', 'core'), split_axis=0, concat_axis...  17.2 us
    unnamed x14, local copies, waits for them, and re-layouts  4.37 us
    ppermute x1, starting transfers between devices, per_device(): other = lax.ppermute(mine, 'core', [(0, 1), (1, 0)])  4.19 us
  transfers between devices with their start and end apart: 2, of which 1 were waited for; matrix products, arithmetic and copies ran while one was open for 0% of the time, Pallas kernels for 1%

profile of v6, /device:TPU:1, one launch (start us, length us, event | category | flops | bytes accessed | tf_op | source)
XLA Modules:
  0.0 168.5 jit_solution(11714116125249104487)
XLA Ops:
  0.6 0.0 copy-start
  0.6 0.9 copy-done
  1.6 0.7 constant_dynamic-slice_fusion
  2.3 17.2 %all-to-all-start = ((bf16[8,64,128]{2,1,0:T(8,128)(2,1)}), bf16[8,64,128]{2,1,0:T(8,128)(2,1)S(1)}, u32[]{:S(2)}, u32[]{:S(2)}) async-start(bf16[8,64,128]{2,1,0:T(8,128)(2,1)} %bitcast.4), calls=%async_computation | async-start | bytes 262144 | tf_op jit(solution)/shard_map/all_to_all | solution.py:375
  19.5 0.0 copy-start.1
  19.5 1.4 copy-done.1
  20.9 0.0 copy-start.4
  20.9 0.7 copy-done.4
  21.6 0.0 copy-start.5
  21.6 0.7 copy-done.5
  22.3 0.0 copy-start.6
  22.3 0.7 copy-done.6
  22.9 1.2 dense_blocks.1.mine.refs_2_
  24.1 0.1 pad_add_fusion.pos.refs_0_
  24.2 3.0 %all-to-all-done.planes = bf16[8,64,128]{2,1,0:T(8,128)(2,1)S(1)} async-done(((bf16[8,64,128]{2,1,0:T(8,128)(2,1)}), bf16[8,64,128]{2,1,0:T(8,128)(2,1)S(1)}, u32[]{:S(2)}, u32[]{:S(2)}) %all-to-all-start) | async-done | bytes 131104 | tf_op jit(solution)/shard_map/all_to_all | solution.py:375
  27.3 0.6 window_pieces.1
  27.9 4.2 %collective-permute-start = (bf16[512,2048]{1,0:T(8,128)(2,1)S(1)}, bf16[512,2048]{1,0:T(8,128)(2,1)S(1)}, u32[]{:S(2)}, u32[]{:S(2)}) collective-permute-start(bf16[512,2048]{1,0:T(8,128)(2,1)S(1)} %dense_blocks.1.mine.refs_2_), channel_id=1, source_target_pairs={{0,1},{1,0},{2,3},{3,2},{4,5},{5,4},{6,7},{7,6},{8,9},{9,8},{10,11... | collective-permute-start | bytes 6291464 | tf_op jit(solution)/shard_map/ppermute | solution.py:404
  32.1 40.2 %all_to_all.39 = bf16[64,64,128]{2,1,0:T(8,128)(2,1)S(1)} all-to-all(bf16[64,64,128]{2,1,0:T(8,128)(2,1)S(1)} %window_pieces.1), channel_id=1, replica_groups={{0,2,4,6,8,10,12,14,16,18,20,22,24,26,28,30,32,34,36,38,40,42,44,46,48,..., dimensions={0} | all-to-all | bytes 2097152 | tf_op jit(solution)/shard_map/all_to_all | solution.py:375
  72.3 0.0 collective-permute-done.other.refs_3_
  72.3 0.0 copy-start.2
  72.3 0.0 copy-start.3
  72.3 1.8 %forward_part.1 = bf16[512,128]{1,0:T(8,128)(2,1)S(1)} custom-call(s32[4]{0:T(128)S(1)} %pad_add_fusion.pos.refs_0_, bf16[512,2048]{1,0:T(8,128)(2,1)S(1)} %dense_blocks.1.mine.refs_2_, bf16[512,2048]{1,0:T(8,128)(2,1)S(1)} %collective-permute-done.other.refs_3_, bf16[8,512,128]{2,1,0:T(8,128)(2,1)S(1)} %bitcast.13), custom_call_target="tpu_custom_call" | custom-call | flops 536870912 | bytes 5242880 | tf_op jit(solution)/shard_map/forward_part/pallas_call | solution.py:106
  74.1 16.1 %all_to_all.40.parts = bf16[16,32,128]{2,1,0:T(8,128)(2,1)S(1)} all-to-all(bf16[16,32,128]{2,1,0:T(8,128)(2,1)S(1)} %bitcast.15), channel_id=1, replica_groups=mesh['z'=8,'y'=8,'x'=8,'core'=2] {'x','core'}, dimensions={0} | all-to-all | bytes 262144 | tf_op jit(solution)/shard_map/all_to_all | solution.py:386
  90.3 0.0 copy-done.2
  90.3 0.0 copy-done.3
  90.3 0.8 layer_part.1
  91.1 14.1 %all_to_all.41.refs_1_ = bf16[16,64,128]{2,1,0:T(8,128)(2,1)S(1)} all-to-all(bf16[16,64,128]{2,1,0:T(8,128)(2,1)S(1)} %get-tuple-element.20), channel_id=1, replica_groups={{0,1,2,3,4,5,6,7,8,9,10,11,12,13,14,15},{16,17,18,19,20,21,22,23,24,25,..., dimensions={0} | all-to-all | bytes 524288 | tf_op jit(solution)/shard_map/all_to_all | solution.py:375
  105.2 1.4 backward_part.1
  106.5 29.2 %all_to_all.42.refs_1_ = bf16[8,544,128]{2,1,0:T(8,128)(2,1)S(1)} all-to-all(bf16[8,544,128]{2,1,0:T(8,128)(2,1)S(1)} %bitcast.12), channel_id=1, replica_groups={{0,16,32,48,64,80,96,112},{2,18,34,50,66,82,98,114},{4,20,36,52,68,84,1..., dimensions={0} | all-to-all | bytes 2228224 | tf_op jit(solution)/shard_map/all_to_all | solution.py:375
  135.8 0.9 merge_part.1
  136.7 13.7 %all_to_all.43.refs_1_ = bf16[8,160,128]{2,1,0:T(8,128)(2,1)S(1)} all-to-all(bf16[8,160,128]{2,1,0:T(8,128)(2,1)S(1)} %merge_part.1), channel_id=1, replica_groups={{1,17,33,49,65,81,97,113},{3,19,35,51,67,83,99,115},{5,21,37,53,69,85,1..., dimensions={0} | all-to-all | bytes 655360 | tf_op jit(solution)/shard_map/all_to_all | solution.py:375
  150.5 0.6 place_part.1
  151.1 16.1 %all_to_all.44.refs_1_ = bf16[16,64,128]{2,1,0:T(8,128)(2,1)S(1)} all-to-all(bf16[16,64,128]{2,1,0:T(8,128)(2,1)S(1)} %place_part.1), channel_id=1, replica_groups=mesh['z'=8,'y'=8,'x'=8,'core'=2] {'z','core'}, dimensions={0} | all-to-all | bytes 524288 | tf_op jit(solution)/shard_map/all_to_all | solution.py:386
  167.2 1.3 finish_part.1
Async XLA Ops:
  0.6 1.0 copy-start
  2.3 25.0 %all-to-all-start = ((bf16[8,64,128]{2,1,0:T(8,128)(2,1)}), bf16[8,64,128]{2,1,0:T(8,128)(2,1)S(1)}, u32[]{:S(2)}, u32[]{:S(2)}) async-start(bf16[8,64,128]{2,1,0:T(8,128)(2,1)} %bitcast.4), calls=%async_computation | async-start | bytes 262144 | tf_op jit(solution)/shard_map/all_to_all | solution.py:375
  19.5 1.4 copy-start.1
  20.9 0.7 copy-start.4
  21.6 0.7 copy-start.5
  22.3 0.7 copy-start.6
  27.9 44.4 %collective-permute-start = (bf16[512,2048]{1,0:T(8,128)(2,1)S(1)}, bf16[512,2048]{1,0:T(8,128)(2,1)S(1)}, u32[]{:S(2)}, u32[]{:S(2)}) collective-permute-start(bf16[512,2048]{1,0:T(8,128)(2,1)S(1)} %dense_blocks.1.mine.refs_2_), channel_id=1, source_target_pairs={{0,1},{1,0},{2,3},{3,2},{4,5},{5,4},{6,7},{7,6},{8,9},{9,8},{10,11... | collective-permute-start | bytes 6291464 | tf_op jit(solution)/shard_map/ppermute | solution.py:404
  72.3 17.9 %copy-start.2 = (bf16[256,256]{1,0:T(8,128)(2,1)S(1)}, bf16[256,256]{1,0:T(8,128)(2,1)}, u32[]{:S(2)}) copy-start(bf16[256,256]{1,0:T(8,128)(2,1)} %weight.1) | copy-start | bytes 393220
  72.3 18.0 %copy-start.3 = (bf16[32,256]{1,0:T(8,128)(2,1)S(1)}, bf16[32,256]{1,0:T(8,128)(2,1)}, u32[]{:S(2)}) copy-start(bf16[32,256]{1,0:T(8,128)(2,1)} %cot.1) | copy-start | bytes 49156

commit v7 on v6

--- a/solution.py
+++ b/solution.py
@@ -59,28 +59,62 @@
     )(rows, cols, count, tiles)
 
 
-def window_kernel(pos, planes, out):
-    ranks = planes.shape[0]
+def light_kernel(pos, planes, out):
+    ranks, share = planes.shape[:2]
+    second_core = pos[3] == 1
+    here = wrap(pos[0] + pos[2], ranks)
     place = [pos[2]]
     for step in range(ranks):
         place.append(wrap(place[-1] + 1, ranks))
-    for target in range(out.shape[0]):
-        section, step = target // ranks, target % ranks
-        out[target] = planes[jnp.where(section > pos[1], place[step + 1], place[step])]
-
-
-def window_pieces(pos, planes, sections):
-    ranks = planes.shape[0]
-    shape = (sections * ranks,) + planes.shape[1:]
-    return pl.pallas_call(
-        window_kernel,
+    for target in range(ranks):
+        ahead = wrap(here + (target > pos[1]).astype(jnp.int32), ranks)
+        out[target, :share, :] = planes[jnp.where(second_core, ahead, place[target])]
+        out[target, share:, :] = planes[place[target + 1]]
+
+
+def light_pieces(pos, planes):
+    ranks, share, width = planes.shape
+    shape = (ranks, 2 * share, width)
+    return pl.pallas_call(
+        light_kernel,
         out_shape=shape_of(shape),
         in_specs=[SMEM, VMEM],
         out_specs=VMEM,
         compiler_params=params(),
         cost_estimate=cost(0, math.prod(shape) * 2),
-        name="window_pieces",
+        name="light_pieces",
     )(pos, planes)
+
+
+def heavy_kernel(pos, parts, out):
+    ranks, height, width = parts.shape
+    share = height // 2
+    near = parts[:, :share, :].reshape(ranks * share, width)
+    for target in range(ranks):
+        out[target] = near
+
+    @pl.when(pos[3] == 0)
+    def _():
+        far = parts[:, share:, :].reshape(ranks * share, width)
+        for target in range(ranks):
+
+            @pl.when(target > pos[1])
+            def _():
+                out[target] = far
+
+
+def heavy_pieces(pos, parts):
+    ranks, height, width = parts.shape
+    shape = (ranks, ranks * height // 2, width)
+    return pl.pallas_call(
+        heavy_kernel,
+        out_shape=shape_of(shape),
+        in_specs=[SMEM, VMEM],
+        out_specs=VMEM,
+        compiler_params=params(),
+        cost_estimate=cost(0, math.prod(shape) * 2),
+        name="heavy_pieces",
+    )(pos, parts)
 
 
 def block_order(pos, sections, own, section):
@@ -89,12 +123,20 @@
 
 
 def forward_kernel(pos, mine, other, blocks, out):
-    sections = blocks.shape[0]
+    rows, width = out.shape
+    sections = blocks.shape[0] // rows
+    share = rows // sections
+    by_block = jnp.where(pos[3] == 0, rows, share)
+    by_slice = jnp.where(pos[3] == 0, share, rows)
     total = None
     for is_own, matrix in ((True, mine), (False, other)):
-        side = jnp.concatenate(
-            [blocks[block_order(pos, sections, is_own, i)] for i in range(sections // 2)], axis=0
-        )
+        slices = []
+        for section in range(sections // 2):
+            first = block_order(pos, sections, is_own, section) * by_block
+            for i in range(sections):
+                start = pl.multiple_of(first + i * by_slice, 16)
+                slices.append(blocks[pl.ds(start, share), :])
+        side = jnp.concatenate(slices, axis=0)
         product = jnp.dot(matrix[...], side, preferred_element_type=F32)
         total = product if total is None else total + product
     out[...] = total.astype(BF16)
@@ -340,23 +382,27 @@
 
 def plane_groups(ranks):
     return [
-        [device_at(ranks, i - rank, section, rank, core) for i in range(ranks)]
+        [device_at(ranks, i - rank * (1 - core), section, rank, core) for i in range(ranks)]
         for section in range(ranks)
         for rank in range(ranks)
         for core in (0, 1)
     ]
 
 
-def window_groups(ranks):
-    return [
-        [
-            device_at(ranks, depth, section, (i - depth) % ranks, core)
-            for section in range(ranks)
-            for i in range(ranks)
-        ]
-        for depth in range(ranks)
-        for core in (0, 1)
-    ]
+def light_groups(ranks):
+    every = [(a, b) for a in range(ranks) for b in range(ranks)]
+    steps = range(ranks)
+    row = [[device_at(ranks, a, b, (i - a) % ranks, 0) for i in steps] for a, b in every]
+    line = [[device_at(ranks, a, k, b, 1) for k in steps] for a, b in every]
+    return row + line
+
+
+def heavy_groups(ranks):
+    every = [(a, b) for a in range(ranks) for b in range(ranks)]
+    steps = range(ranks)
+    line = [[device_at(ranks, a, k, b, 0) for k in steps] for a, b in every]
+    slant = [[device_at(ranks, i, b, (a - i) % ranks, 1) for i in steps] for a, b in every]
+    return line + slant
 
 
 def replica_groups(ranks):
@@ -400,10 +446,12 @@
     )
     planes = grouped(half.reshape(ranks, share, width), plane_groups(ranks))
     mine = dense_blocks(tile_values[0], tile_rows[0], tile_cols[0], tile_count[0], rows)
-    pieces, mine = lax.optimization_barrier((window_pieces(pos, planes, ranks), mine))
+    pieces, mine = lax.optimization_barrier((light_pieces(pos, planes), mine))
     other = lax.ppermute(mine, "core", [(0, 1), (1, 0)])
-    blocks = grouped(pieces, window_groups(ranks))
-    part = forward_part(pos, mine, other, blocks.reshape(ranks, rows, width))
+    parts = grouped(pieces, light_groups(ranks))
+    pieces, other = lax.optimization_barrier((heavy_pieces(pos, parts), other))
+    blocks = grouped(pieces, heavy_groups(ranks))
+    part = forward_part(pos, mine, other, blocks.reshape(ranks * rows, width))
     parts = exchange(part.reshape(2 * ranks, own, width), ("x", "core"))
     activations, pieces = layer_part(parts, cotangent, weight)
     parts = grouped(pieces, replica_groups(ranks))

time: 169 us -> 171 us (1.012)
    all_to_all x4 -> x5, blocking collectives: 97.3 us -> 103 us  [grouped(): lax.all_to_all(pieces, ('z', 'y', 'x', 'core'), split_axis=0, concat_axis...]
    all_to_all x2, blocking collectives: 32.3 us -> 27.5 us  [exchange(): return lax.all_to_all(pieces, axis, split_axis=0, concat_axis=0, tiled=True)]
where the time goes in v7:
time: 171 us; the launch traced here: 170 us
  blocking collectives  131 us (77%)
  starting transfers between devices  21.4 us (13%)
  Pallas kernels  9.44 us (6%)
  local copies, waits for them, and re-layouts  5.04 us (3%)
  waiting for transfers between devices  2.89 us (2%)
    all_to_all x5, blocking collectives, grouped(): lax.all_to_all(pieces, ('z', 'y', 'x', 'core'), split_axis=0, concat_axis...  103 us
    all_to_all x2, blocking collectives, exchange(): return lax.all_to_all(pieces, axis, split_axis=0, concat_axis=0, tiled=True)  27.5 us
    all_to_all x1, starting transfers between devices, grouped(): lax.all_to_all(pieces, ('z', 'y', 'x', 'core'), split_axis=0, concat_axis...  17.2 us
    unnamed x14, local copies, waits for them, and re-layouts  4.37 us
    ppermute x1, starting transfers between devices, per_device(): other = lax.ppermute(mine, 'core', [(0, 1), (1, 0)])  4.19 us
  transfers between devices with their start and end apart: 2, of which 1 were waited for; matrix products, arithmetic and copies ran while one was open for 0% of the time, Pallas kernels for 1%

profile of v7, /device:TPU:1, one launch (start us, length us, event | category | flops | bytes accessed | tf_op | source)
XLA Modules:
  0.0 170.4 jit_solution(2212558291682590823)
XLA Ops:
  0.6 0.0 copy-start
  0.6 0.9 copy-done
  1.6 0.7 constant_dynamic-slice_fusion
  2.3 17.2 %all-to-all-start = ((bf16[8,64,128]{2,1,0:T(8,128)(2,1)}), bf16[8,64,128]{2,1,0:T(8,128)(2,1)S(1)}, u32[]{:S(2)}, u32[]{:S(2)}) async-start(bf16[8,64,128]{2,1,0:T(8,128)(2,1)} %bitcast.4), calls=%async_computation | async-start | bytes 262144 | tf_op jit(solution)/shard_map/all_to_all | solution.py:421
  19.5 0.0 copy-start.1
  19.5 1.4 copy-done.1
  20.9 0.0 copy-start.4
  20.9 0.7 copy-done.4
  21.6 0.0 copy-start.5
  21.6 0.7 copy-done.5
  22.3 0.0 copy-start.6
  22.3 0.7 copy-done.6
  22.9 1.4 dense_blocks.1.mine.refs_2_
  24.3 0.1 pad_add_fusion.pos.refs_0_
  24.4 2.9 %all-to-all-done.planes = bf16[8,64,128]{2,1,0:T(8,128)(2,1)S(1)} async-done(((bf16[8,64,128]{2,1,0:T(8,128)(2,1)}), bf16[8,64,128]{2,1,0:T(8,128)(2,1)S(1)}, u32[]{:S(2)}, u32[]{:S(2)}) %all-to-all-start) | async-done | bytes 131104 | tf_op jit(solution)/shard_map/all_to_all | solution.py:421
  27.3 0.6 light_pieces.1
  27.8 4.2 %collective-permute-start = (bf16[512,2048]{1,0:T(8,128)(2,1)S(1)}, bf16[512,2048]{1,0:T(8,128)(2,1)S(1)}, u32[]{:S(2)}, u32[]{:S(2)}) collective-permute-start(bf16[512,2048]{1,0:T(8,128)(2,1)S(1)} %dense_blocks.1.mine.refs_2_), channel_id=1, source_target_pairs={{0,1},{1,0},{2,3},{3,2},{4,5},{5,4},{6,7},{7,6},{8,9},{9,8},{10,11... | collective-permute-start | bytes 6291464 | tf_op jit(solution)/shard_map/ppermute | solution.py:450
  32.0 16.4 %all_to_all.44.parts = bf16[8,128,128]{2,1,0:T(8,128)(2,1)S(1)} all-to-all(bf16[8,128,128]{2,1,0:T(8,128)(2,1)S(1)} %light_pieces.1), channel_id=1, replica_groups={{0,2,4,6,8,10,12,14},{16,18,20,22,24,26,28,30},{32,34,36,38,40,42,44,46..., dimensions={0} | all-to-all | bytes 524288 | tf_op jit(solution)/shard_map/all_to_all | solution.py:421
  48.4 0.7 heavy_pieces.1
  49.1 0.0 collective-permute-done.other.refs_3_
  49.1 31.0 %all_to_all.45 = bf16[8,512,128]{2,1,0:T(8,128)(2,1)S(1)} all-to-all(bf16[8,512,128]{2,1,0:T(8,128)(2,1)S(1)} %heavy_pieces.1), channel_id=1, replica_groups={{0,16,32,48,64,80,96,112},{2,18,34,50,66,82,98,114},{4,20,36,52,68,84,1..., dimensions={0} | all-to-all | bytes 2097152 | tf_op jit(solution)/shard_map/all_to_all | solution.py:421
  80.1 0.0 copy-start.2
  80.1 0.0 copy-start.3
  80.1 1.8 %forward_part.1 = bf16[512,128]{1,0:T(8,128)(2,1)S(1)} custom-call(s32[4]{0:T(128)S(1)} %pad_add_fusion.pos.refs_0_, bf16[512,2048]{1,0:T(8,128)(2,1)S(1)} %dense_blocks.1.mine.refs_2_, bf16[512,2048]{1,0:T(8,128)(2,1)S(1)} %collective-permute-done.other.refs_3_, bf16[4096,128]{1,0:T(8,128)(2,1)S(1)} %bitcast.13), custom_call_target="tpu_custom_call" | custom-call | flops 536870912 | bytes 5242880 | tf_op jit(solution)/shard_map/forward_part/pallas_call | solution.py:148
  81.9 10.5 %all_to_all.46.parts = bf16[16,32,128]{2,1,0:T(8,128)(2,1)S(1)} all-to-all(bf16[16,32,128]{2,1,0:T(8,128)(2,1)S(1)} %bitcast.15), channel_id=1, replica_groups=mesh['z'=8,'y'=8,'x'=8,'core'=2] {'x','core'}, dimensions={0} | all-to-all | bytes 262144 | tf_op jit(solution)/shard_map/all_to_all | solution.py:432
  92.4 0.0 copy-done.2
  92.4 0.0 copy-done.3
  92.4 0.8 layer_part.1
  93.2 14.4 %all_to_all.47.refs_1_ = bf16[16,64,128]{2,1,0:T(8,128)(2,1)S(1)} all-to-all(bf16[16,64,128]{2,1,0:T(8,128)(2,1)S(1)} %get-tuple-element.24), channel_id=1, replica_groups={{0,1,2,3,4,5,6,7,8,9,10,11,12,13,14,15},{16,17,18,19,20,21,22,23,24,25,..., dimensions={0} | all-to-all | bytes 524288 | tf_op jit(solution)/shard_map/all_to_all | solution.py:421
  107.6 1.4 backward_part.1
  109.0 28.8 %all_to_all.48.refs_1_ = bf16[8,544,128]{2,1,0:T(8,128)(2,1)S(1)} all-to-all(bf16[8,544,128]{2,1,0:T(8,128)(2,1)S(1)} %bitcast.12), channel_id=1, replica_groups={{0,16,32,48,64,80,96,112},{2,18,34,50,66,82,98,114},{4,20,36,52,68,84,1..., dimensions={0} | all-to-all | bytes 2228224 | tf_op jit(solution)/shard_map/all_to_all | solution.py:421
  137.8 0.9 merge_part.1
  138.7 12.7 %all_to_all.49.refs_1_ = bf16[8,160,128]{2,1,0:T(8,128)(2,1)S(1)} all-to-all(bf16[8,160,128]{2,1,0:T(8,128)(2,1)S(1)} %merge_part.1), channel_id=1, replica_groups={{1,17,33,49,65,81,97,113},{3,19,35,51,67,83,99,115},{5,21,37,53,69,85,1..., dimensions={0} | all-to-all | bytes 655360 | tf_op jit(solution)/shard_map/all_to_all | solution.py:421
  151.4 0.6 place_part.1
  152.0 17.0 %all_to_all.50.refs_1_ = bf16[16,64,128]{2,1,0:T(8,128)(2,1)S(1)} all-to-all(bf16[16,64,128]{2,1,0:T(8,128)(2,1)S(1)} %place_part.1), channel_id=1, replica_groups=mesh['z'=8,'y'=8,'x'=8,'core'=2] {'z','core'}, dimensions={0} | all-to-all | bytes 524288 | tf_op jit(solution)/shard_map/all_to_all | solution.py:432
  169.1 1.3 finish_part.1
Async XLA Ops:
  0.6 1.0 copy-start
  2.3 25.0 %all-to-all-start = ((bf16[8,64,128]{2,1,0:T(8,128)(2,1)}), bf16[8,64,128]{2,1,0:T(8,128)(2,1)S(1)}, u32[]{:S(2)}, u32[]{:S(2)}) async-start(bf16[8,64,128]{2,1,0:T(8,128)(2,1)} %bitcast.4), calls=%async_computation | async-start | bytes 262144 | tf_op jit(solution)/shard_map/all_to_all | solution.py:421
  19.5 1.4 copy-start.1
  20.9 0.7 copy-start.4
  21.6 0.7 copy-start.5
  22.3 0.7 copy-start.6
  27.8 21.3 %collective-permute-start = (bf16[512,2048]{1,0:T(8,128)(2,1)S(1)}, bf16[512,2048]{1,0:T(8,128)(2,1)S(1)}, u32[]{:S(2)}, u32[]{:S(2)}) collective-permute-start(bf16[512,2048]{1,0:T(8,128)(2,1)S(1)} %dense_blocks.1.mine.refs_2_), channel_id=1, source_target_pairs={{0,1},{1,0},{2,3},{3,2},{4,5},{5,4},{6,7},{7,6},{8,9},{9,8},{10,11... | collective-permute-start | bytes 6291464 | tf_op jit(solution)/shard_map/ppermute | solution.py:450
  80.1 12.3 %copy-start.2 = (bf16[256,256]{1,0:T(8,128)(2,1)S(1)}, bf16[256,256]{1,0:T(8,128)(2,1)}, u32[]{:S(2)}) copy-start(bf16[256,256]{1,0:T(8,128)(2,1)} %weight.1) | copy-start | bytes 393220
  80.1 12.3 %copy-start.3 = (bf16[32,256]{1,0:T(8,128)(2,1)S(1)}, bf16[32,256]{1,0:T(8,128)(2,1)}, u32[]{:S(2)}) copy-start(bf16[32,256]{1,0:T(8,128)(2,1)} %cot.1) | copy-start | bytes 49156
